TPU v7x, 32 devices: a whole 2x2x4 slice. The times are simulated.
32 devices in a mesh: dp: 8 (over z, core), tensor: 4 (over y, x).
Axes of the slice: x: 2, y: 2, z: 4, core: 2. Of those that a mesh axis runs over, the one named last changes fastest.
Arguments:
- queries: bfloat16 [4096, 4096], P('dp')
- keys: bfloat16 [4096, 4096], P('dp')
- projection: bfloat16 [4096, 1024], P(None, 'tensor'), may hold values from -0.09375 to 0.09375
- positives: int32 [8, 512], P('dp'), may hold values from 0 to 511, each once within a row
Outputs:
- pair_loss: float32 [4096], P(('dp', 'tensor'))
- grad_queries: float32 [4096, 1024], P(('dp', 'tensor'))
- grad_keys: float32 [4096, 1024], P(('dp', 'tensor'))
Inputs may be any that keep to these rules, and one draw needn't show every extreme that they name: Each row of positives holds every number of 0 to 511 once.
All inputs are finite; a program needn't handle non-finite values.
Results may differ from a plain program's by a relative error of at most 0.0069.
Values may be sent and summed in bfloat16 or wider, within the bound.
A program may use at most 128 MiB of HBM per device.

v0:
```python
import jax
import jax.numpy as jnp
from jax import lax
from jax.sharding import PartitionSpec as P

SCALE = 100.0
EPSILON = 1e-06


def shifted(value, axis, steps):
    count = lax.axis_size(axis)
    pairs = [(source, (source + steps) % count) for source in range(count)]
    return lax.ppermute(value, axis, pairs)


def combined_all(part, axis, combine):
    gathered = jax.tree.map(lambda a: lax.all_gather(a, axis), part)

    def take(source):
        return jax.tree.map(lambda a: lax.dynamic_index_in_dim(a, source, 0, False), gathered)

    return lax.fori_loop(
        1, lax.axis_size(axis), lambda source, state: combine(state, take(source)), take(0)
    )


def normalize(embedding):
    entries = embedding.astype(jnp.float32)
    magnitude = jnp.sqrt(jnp.sum(entries * entries, axis=1, keepdims=True) + EPSILON)
    return (entries / magnitude, magnitude)


def unnormalize(grad_unit, unit_rows, magnitude):
    return (
        grad_unit - unit_rows * jnp.sum(unit_rows * grad_unit, axis=1, keepdims=True)
    ) / magnitude


def similarity(queries_unit, key_block):
    return SCALE * lax.dot_general(
        queries_unit, key_block, (((1,), (1,)), ((), ())), preferred_element_type=jnp.float32
    )


def cycle_keys(block, offset):
    return shifted(block, "dp", offset)


def cycle_grads(partial_value, offset):
    return shifted(partial_value, "dp", offset)


def advance(keys_now, direction):
    result = cycle_keys(keys_now, direction)
    return result


def absorb(running, queries_unit, key_block):
    row_max, row_sum = running
    scores = similarity(queries_unit, key_block)
    new_max = jnp.maximum(row_max, jnp.max(scores, axis=1))
    row_sum = row_sum * jnp.exp(row_max - new_max) + jnp.sum(
        jnp.exp(scores - new_max[:, None]), axis=1
    )
    return (new_max, row_sum)


def combine(earlier, latter):
    new_max = jnp.maximum(earlier[0], latter[0])
    row_sum = earlier[1] * jnp.exp(earlier[0] - new_max) + latter[1] * jnp.exp(latter[0] - new_max)
    return (new_max, row_sum, earlier[2] + latter[2])


def contributions(queries_unit, key_block, log_total, positive_mask):
    scores = similarity(queries_unit, key_block)
    weights = (jnp.exp(scores - log_total[:, None]) - positive_mask).astype(jnp.bfloat16)
    grad_q = SCALE * jnp.dot(weights, key_block, preferred_element_type=jnp.float32)
    grad_k = SCALE * lax.dot_general(
        weights, queries_unit, (((0,), (0,)), ((), ())), preferred_element_type=jnp.float32
    )
    return (grad_q, grad_k)


def body(queries, keys, projection, positives):
    query_count = queries.shape[0]
    group_count = lax.axis_size("tensor")
    cycle_count = lax.axis_size("dp")
    group_index = lax.axis_index("tensor")
    key_rows = query_count // group_count
    query_part = jnp.dot(queries, projection, preferred_element_type=jnp.float32).astype(
        jnp.bfloat16
    )
    key_part = jnp.dot(keys, projection, preferred_element_type=jnp.float32).astype(jnp.bfloat16)
    query_full, key_full = (
        lax.all_gather(query_part, "tensor", axis=1, tiled=True),
        lax.all_gather(key_part, "tensor", axis=1, tiled=True),
    )
    query_unit, query_mag = normalize(query_full)
    queries_unit = query_unit.astype(jnp.bfloat16)
    row_start = group_index * key_rows
    key_unit, key_mag = normalize(lax.dynamic_slice_in_dim(key_full, row_start, key_rows, 0))
    key_block = key_unit.astype(jnp.bfloat16)
    target = positives[0] - row_start
    positive_mask = (
        lax.broadcasted_iota(jnp.int32, (query_count, key_rows), 1) == target[:, None]
    ).astype(jnp.float32)
    own_scores = similarity(queries_unit, key_block)
    row_max = jnp.max(own_scores, axis=1)
    row_sum = jnp.sum(jnp.exp(own_scores - row_max[:, None]), axis=1)
    matched = jnp.sum(own_scores * positive_mask, axis=1)

    def step_ahead(keys_now):
        return advance(keys_now, 1)

    def sweep_one(turn_number, carried):
        forward_keys, running = carried
        forward_keys = step_ahead(forward_keys)
        return (forward_keys, absorb(running, queries_unit, forward_keys))

    forward_keys, running = lax.fori_loop(
        0, cycle_count - 1, sweep_one, (key_block, (row_max, row_sum))
    )
    row_max, row_sum, matched = combined_all((running[0], running[1], matched), "tensor", combine)
    log_total = row_max + jnp.log(row_sum)
    pair_loss = lax.dynamic_slice_in_dim(log_total - matched, row_start, key_rows, 0)
    grad_q, own_grad_k = contributions(queries_unit, key_block, log_total, positive_mask)

    def visit_one(turn_number, carried):
        forward_keys, forward_total, grad_sum = carried
        forward_keys = step_ahead(forward_keys)
        forward_total = cycle_grads(forward_total, 1)
        ahead_q, ahead_k = contributions(queries_unit, forward_keys, log_total, 0.0)
        return (forward_keys, forward_total + ahead_k, grad_sum + ahead_q)

    forward_keys, forward_total, grad_q = lax.fori_loop(
        0, cycle_count - 1, visit_one, (key_block, own_grad_k, grad_q)
    )
    grad_key_hat = cycle_grads(forward_total, 1)
    grad_rows = lax.psum_scatter(grad_q, "tensor", scatter_dimension=0, tiled=True)
    unit_rows = lax.dynamic_slice_in_dim(query_unit, row_start, key_rows, 0)
    magnitude_rows = lax.dynamic_slice_in_dim(query_mag, row_start, key_rows, 0)
    grad_queries = unnormalize(grad_rows, unit_rows, magnitude_rows)
    grad_keys = unnormalize(grad_key_hat, key_unit, key_mag)
    return (pair_loss, grad_queries, grad_keys)


def solution(mesh):
    in_specs = (P("dp", None), P("dp", None), P(None, "tensor"), P("dp", None))
    out_specs = (P(("dp", "tensor")), P(("dp", "tensor"), None), P(("dp", "tensor"), None))
    return jax.shard_map(body, mesh=mesh, in_specs=in_specs, out_specs=out_specs, check_vma=False)
```

profile of v0, /device:TPU:0, one launch (start us, length us, event | category | flops | bytes accessed | tf_op | source)
XLA Modules:
  0.0 323.2 jit_solution(1152912538256923707)
XLA Ops:
  8.8 4.1 %convolution_convert_fusion = bf16[512,256]{1,0:T(8,128)(2,1)} fusion(bf16[512,4096]{1,0:T(8,128)(2,1)} %param.10, bf16[4096,256]{1,0:T(8,128)(2,1)S(1)} %copy-done), kind=kOutput, calls=%fused_computation.19 | convolution fusion | flops 1073872896 | bytes 6553600 | tf_op jit(solution)/shard_map/dot_general | solution.py:90
  13.0 4.1 %convolution_convert_fusion.1 = bf16[512,256]{1,0:T(8,128)(2,1)} fusion(bf16[512,4096]{1,0:T(8,128)(2,1)} %param.11, bf16[4096,256]{1,0:T(8,128)(2,1)S(1)} %copy-done), kind=kOutput, calls=%fused_computation.20 | convolution fusion | flops 1073872896 | bytes 6553600 | tf_op jit(solution)/shard_map/dot_general | solution.py:93
  17.2 25.0 %all-gather.11.cloned.1.call-done = bf16[512,1024]{1,0:T(8,128)(2,1)} async-done(((bf16[512,256]{1,0:T(8,128)(2,1)}), bf16[512,1024]{1,0:T(8,128)(2,1)}) %all-gather.11.cloned.1.call-update) | async-done | bytes 1048592 | tf_op jit(solution)/shard_map/all_gather | solution.py:95
  43.8 27.4 %all-gather.9.cloned.1.call-done = bf16[512,1024]{1,0:T(8,128)(2,1)} async-done(((bf16[512,256]{1,0:T(8,128)(2,1)}), bf16[512,1024]{1,0:T(8,128)(2,1)}) %all-gather.9.cloned.1.call-update) | async-done | bytes 1048592 | tf_op jit(solution)/shard_map/all_gather | solution.py:96
  78.4 63.9 %while.47 = (s32[]{:T(128)}, bf16[128,1024]{1,0:T(8,128)(2,1)}, f32[512]{0:T(512)S(1)}, f32[512]{0:T(512)S(1)}, bf16[512,1024]{1,0:T(8,128)(2,1)S(1)}, /*index=5*/s32[]{:T(128)}) while((s32[]{:T(128)}, bf16[128,1024]{1,0:T(8,128)(2,1)}, f32[512]{0:T(512)S(1)}, f32[512]{0:T(512)S(1)}, bf16[512,1024]{1,0:T(8,128)(2,1)S(1)}, ...), condition=%wide.region_7.8_spmd, body=%wide.region_4.7_spmd.sunk | while | flops 134480896 | bytes 3434605 | solution.py:120
  78.5 7.8 %collective-permute-done = bf16[128,1024]{1,0:T(8,128)(2,1)S(1)} collective-permute-done((bf16[128,1024]{1,0:T(8,128)(2,1)}, bf16[128,1024]{1,0:T(8,128)(2,1)S(1)}, u32[]{:S(2)}, u32[]{:S(2)}) %collective-permute-start) | collective-permute-done | bytes 262176 | tf_op jit(solution)/shard_map/while/body/eval_jaxpr/ppermute | solution.py:13
  87.6 7.8 %collective-permute-done = bf16[128,1024]{1,0:T(8,128)(2,1)S(1)} collective-permute-done((bf16[128,1024]{1,0:T(8,128)(2,1)}, bf16[128,1024]{1,0:T(8,128)(2,1)S(1)}, u32[]{:S(2)}, u32[]{:S(2)}) %collective-permute-start) | collective-permute-done | bytes 262176 | tf_op jit(solution)/shard_map/while/body/eval_jaxpr/ppermute | solution.py:13
  96.7 7.8 %collective-permute-done = bf16[128,1024]{1,0:T(8,128)(2,1)S(1)} collective-permute-done((bf16[128,1024]{1,0:T(8,128)(2,1)}, bf16[128,1024]{1,0:T(8,128)(2,1)S(1)}, u32[]{:S(2)}, u32[]{:S(2)}) %collective-permute-start) | collective-permute-done | bytes 262176 | tf_op jit(solution)/shard_map/while/body/eval_jaxpr/ppermute | solution.py:13
  105.8 7.8 %collective-permute-done = bf16[128,1024]{1,0:T(8,128)(2,1)S(1)} collective-permute-done((bf16[128,1024]{1,0:T(8,128)(2,1)}, bf16[128,1024]{1,0:T(8,128)(2,1)S(1)}, u32[]{:S(2)}, u32[]{:S(2)}) %collective-permute-start) | collective-permute-done | bytes 262176 | tf_op jit(solution)/shard_map/while/body/eval_jaxpr/ppermute | solution.py:13
  114.9 7.8 %collective-permute-done = bf16[128,1024]{1,0:T(8,128)(2,1)S(1)} collective-permute-done((bf16[128,1024]{1,0:T(8,128)(2,1)}, bf16[128,1024]{1,0:T(8,128)(2,1)S(1)}, u32[]{:S(2)}, u32[]{:S(2)}) %collective-permute-start) | collective-permute-done | bytes 262176 | tf_op jit(solution)/shard_map/while/body/eval_jaxpr/ppermute | solution.py:13
  124.0 7.8 %collective-permute-done = bf16[128,1024]{1,0:T(8,128)(2,1)S(1)} collective-permute-done((bf16[128,1024]{1,0:T(8,128)(2,1)}, bf16[128,1024]{1,0:T(8,128)(2,1)S(1)}, u32[]{:S(2)}, u32[]{:S(2)}) %collective-permute-start) | collective-permute-done | bytes 262176 | tf_op jit(solution)/shard_map/while/body/eval_jaxpr/ppermute | solution.py:13
  133.2 7.8 %collective-permute-done = bf16[128,1024]{1,0:T(8,128)(2,1)S(1)} collective-permute-done((bf16[128,1024]{1,0:T(8,128)(2,1)}, bf16[128,1024]{1,0:T(8,128)(2,1)S(1)}, u32[]{:S(2)}, u32[]{:S(2)}) %collective-permute-start) | collective-permute-done | bytes 262176 | tf_op jit(solution)/shard_map/while/body/eval_jaxpr/ppermute | solution.py:13
  142.3 8.1 %all-gather.4 = f32[4,1,512]{2,1,0:T(1,128)S(1)} all-gather(f32[1,1,512]{2,1,0:T(1,128)S(1)} %bitcast.61), channel_id=3, replica_groups=mesh['dp'=8,'tensor'=4] {'tensor'}, dimensions={0}, use_global_device_ids=true | all-gather | bytes 10240 | tf_op jit(solution)/shard_map/all_gather | solution.py:17
  150.4 7.1 %all-gather.3 = f32[4,1,512]{2,1,0:T(1,128)S(1)} all-gather(f32[1,1,512]{2,1,0:T(1,128)S(1)} %bitcast.57), channel_id=2, replica_groups=mesh['dp'=8,'tensor'=4] {'tensor'}, dimensions={0}, use_global_device_ids=true | all-gather | bytes 10240 | tf_op jit(solution)/shard_map/all_gather | solution.py:17
  157.5 8.0 %all-gather.5 = f32[4,1,512]{2,1,0:T(1,128)S(1)} all-gather(f32[1,1,512]{2,1,0:T(1,128)S(1)} %bitcast.71), channel_id=4, replica_groups=mesh['dp'=8,'tensor'=4] {'tensor'}, dimensions={0}, use_global_device_ids=true | all-gather | bytes 10240 | tf_op jit(solution)/shard_map/all_gather | solution.py:17
  170.6 109.9 %while.49 = (s32[]{:T(128)}, bf16[128,1024]{1,0:T(8,128)(2,1)}, f32[128,1024]{1,0:T(8,128)}, f32[512,1024]{1,0:T(8,128)}, bf16[512,1024]{1,0:T(8,128)(2,1)S(1)}, /*index=5*/f32[512]{0:T(512)S(1)}, s32[]{:T(128)}) while((s32[]{:T(128)}, bf16[128,1024]{1,0:T(8,128)(2,1)}, f32[128,1024]{1,0:T(8,128)}, f32[512,1024]{1,0:T(8,128)}, ...), condition=%wide.region_12.13_spmd, body=%wide.region_11.12_spmd.sunk | while | flops 404160512 | bytes 11929757 | solution.py:135
  170.6 7.8 %collective-permute-done.1 = bf16[128,1024]{1,0:T(8,128)(2,1)S(1)} collective-permute-done((bf16[128,1024]{1,0:T(8,128)(2,1)}, bf16[128,1024]{1,0:T(8,128)(2,1)S(1)}, u32[]{:S(2)}, u32[]{:S(2)}) %collective-permute-start.1) | collective-permute-done | bytes 262176 | tf_op jit(solution)/shard_map/while/body/eval_jaxpr/ppermute | solution.py:13
  179.6 3.3 %multiply_add_fusion.8 = f32[512,1024]{1,0:T(8,128)} fusion(f32[512,1024]{1,0:T(8,128)} %get-tuple-element.480, bf16[512,128]{1,0:T(8,128)(2,1)S(1)} %fusion.47, bf16[128,1024]{1,0:T(8,128)(2,1)S(1)} %collective-permute-done.1), kind=kOutput, calls=%fused_computation.7.clone.1 | convolution fusion | flops 135266304 | bytes 4587520 | tf_op jit(solution)/shard_map/while/body/eval_jaxpr/dot_general | solution.py:77
  186.3 7.8 %collective-permute-done.1 = bf16[128,1024]{1,0:T(8,128)(2,1)S(1)} collective-permute-done((bf16[128,1024]{1,0:T(8,128)(2,1)}, bf16[128,1024]{1,0:T(8,128)(2,1)S(1)}, u32[]{:S(2)}, u32[]{:S(2)}) %collective-permute-start.1) | collective-permute-done | bytes 262176 | tf_op jit(solution)/shard_map/while/body/eval_jaxpr/ppermute | solution.py:13
  195.3 3.3 %multiply_add_fusion.8 = f32[512,1024]{1,0:T(8,128)} fusion(f32[512,1024]{1,0:T(8,128)} %get-tuple-element.480, bf16[512,128]{1,0:T(8,128)(2,1)S(1)} %fusion.47, bf16[128,1024]{1,0:T(8,128)(2,1)S(1)} %collective-permute-done.1), kind=kOutput, calls=%fused_computation.7.clone.1 | convolution fusion | flops 135266304 | bytes 4587520 | tf_op jit(solution)/shard_map/while/body/eval_jaxpr/dot_general | solution.py:77
  202.0 7.8 %collective-permute-done.1 = bf16[128,1024]{1,0:T(8,128)(2,1)S(1)} collective-permute-done((bf16[128,1024]{1,0:T(8,128)(2,1)}, bf16[128,1024]{1,0:T(8,128)(2,1)S(1)}, u32[]{:S(2)}, u32[]{:S(2)}) %collective-permute-start.1) | collective-permute-done | bytes 262176 | tf_op jit(solution)/shard_map/while/body/eval_jaxpr/ppermute | solution.py:13
  211.0 3.3 %multiply_add_fusion.8 = f32[512,1024]{1,0:T(8,128)} fusion(f32[512,1024]{1,0:T(8,128)} %get-tuple-element.480, bf16[512,128]{1,0:T(8,128)(2,1)S(1)} %fusion.47, bf16[128,1024]{1,0:T(8,128)(2,1)S(1)} %collective-permute-done.1), kind=kOutput, calls=%fused_computation.7.clone.1 | convolution fusion | flops 135266304 | bytes 4587520 | tf_op jit(solution)/shard_map/while/body/eval_jaxpr/dot_general | solution.py:77
  217.7 7.8 %collective-permute-done.1 = bf16[128,1024]{1,0:T(8,128)(2,1)S(1)} collective-permute-done((bf16[128,1024]{1,0:T(8,128)(2,1)}, bf16[128,1024]{1,0:T(8,128)(2,1)S(1)}, u32[]{:S(2)}, u32[]{:S(2)}) %collective-permute-start.1) | collective-permute-done | bytes 262176 | tf_op jit(solution)/shard_map/while/body/eval_jaxpr/ppermute | solution.py:13
  226.7 3.3 %multiply_add_fusion.8 = f32[512,1024]{1,0:T(8,128)} fusion(f32[512,1024]{1,0:T(8,128)} %get-tuple-element.480, bf16[512,128]{1,0:T(8,128)(2,1)S(1)} %fusion.47, bf16[128,1024]{1,0:T(8,128)(2,1)S(1)} %collective-permute-done.1), kind=kOutput, calls=%fused_computation.7.clone.1 | convolution fusion | flops 135266304 | bytes 4587520 | tf_op jit(solution)/shard_map/while/body/eval_jaxpr/dot_general | solution.py:77
  233.4 7.8 %collective-permute-done.1 = bf16[128,1024]{1,0:T(8,128)(2,1)S(1)} collective-permute-done((bf16[128,1024]{1,0:T(8,128)(2,1)}, bf16[128,1024]{1,0:T(8,128)(2,1)S(1)}, u32[]{:S(2)}, u32[]{:S(2)}) %collective-permute-start.1) | collective-permute-done | bytes 262176 | tf_op jit(solution)/shard_map/while/body/eval_jaxpr/ppermute | solution.py:13
  242.4 3.3 %multiply_add_fusion.8 = f32[512,1024]{1,0:T(8,128)} fusion(f32[512,1024]{1,0:T(8,128)} %get-tuple-element.480, bf16[512,128]{1,0:T(8,128)(2,1)S(1)} %fusion.47, bf16[128,1024]{1,0:T(8,128)(2,1)S(1)} %collective-permute-done.1), kind=kOutput, calls=%fused_computation.7.clone.1 | convolution fusion | flops 135266304 | bytes 4587520 | tf_op jit(solution)/shard_map/while/body/eval_jaxpr/dot_general | solution.py:77
  249.1 7.8 %collective-permute-done.1 = bf16[128,1024]{1,0:T(8,128)(2,1)S(1)} collective-permute-done((bf16[128,1024]{1,0:T(8,128)(2,1)}, bf16[128,1024]{1,0:T(8,128)(2,1)S(1)}, u32[]{:S(2)}, u32[]{:S(2)}) %collective-permute-start.1) | collective-permute-done | bytes 262176 | tf_op jit(solution)/shard_map/while/body/eval_jaxpr/ppermute | solution.py:13
  258.1 3.3 %multiply_add_fusion.8 = f32[512,1024]{1,0:T(8,128)} fusion(f32[512,1024]{1,0:T(8,128)} %get-tuple-element.480, bf16[512,128]{1,0:T(8,128)(2,1)S(1)} %fusion.47, bf16[128,1024]{1,0:T(8,128)(2,1)S(1)} %collective-permute-done.1), kind=kOutput, calls=%fused_computation.7.clone.1 | convolution fusion | flops 135266304 | bytes 4587520 | tf_op jit(solution)/shard_map/while/body/eval_jaxpr/dot_general | solution.py:77
  264.8 7.8 %collective-permute-done.1 = bf16[128,1024]{1,0:T(8,128)(2,1)S(1)} collective-permute-done((bf16[128,1024]{1,0:T(8,128)(2,1)}, bf16[128,1024]{1,0:T(8,128)(2,1)S(1)}, u32[]{:S(2)}, u32[]{:S(2)}) %collective-permute-start.1) | collective-permute-done | bytes 262176 | tf_op jit(solution)/shard_map/while/body/eval_jaxpr/ppermute | solution.py:13
  273.8 3.3 %multiply_add_fusion.8 = f32[512,1024]{1,0:T(8,128)} fusion(f32[512,1024]{1,0:T(8,128)} %get-tuple-element.480, bf16[512,128]{1,0:T(8,128)(2,1)S(1)} %fusion.47, bf16[128,1024]{1,0:T(8,128)(2,1)S(1)} %collective-permute-done.1), kind=kOutput, calls=%fused_computation.7.clone.1 | convolution fusion | flops 135266304 | bytes 4587520 | tf_op jit(solution)/shard_map/while/body/eval_jaxpr/dot_general | solution.py:77
  282.2 9.7 %collective-permute-done.3 = f32[128,1024]{1,0:T(8,128)S(1)} collective-permute-done((f32[128,1024]{1,0:T(8,128)S(1)}, f32[128,1024]{1,0:T(8,128)S(1)}, u32[]{:S(2)}, u32[]{:S(2)}) %collective-permute-start.3) | collective-permute-done | bytes 524320 | tf_op jit(solution)/shard_map/ppermute | solution.py:13
  295.1 18.1 %reduce-scatter.2.cloned.1.call-done = f32[128,1024]{1,0:T(8,128)} async-done(((f32[512,1024]{1,0:T(8,128)}), f32[128,1024]{1,0:T(8,128)}) %reduce-scatter.2.cloned.1.call-update) | async-done | bytes 524304 | tf_op jit(solution)/shard_map/reduce_scatter | solution.py:139
  (148 shorter events, 65.1 us)
Async XLA Ops:
  7.2 1.6 copy-start
  7.2 35.1 %all-gather.11.cloned.1.call-start = ((), (), s32[]{:S(2)}) async-start(), calls=%async_computation.2 | async-start | bytes 1310720 | tf_op jit(solution)/shard_map/all_gather | solution.py:95
  12.9 4.3 %copy-start.5 = (s32[1,512]{1,0:T(1,128)S(1)}, s32[1,512]{1,0:T(1,128)}, u32[]{:S(2)}) copy-start(s32[1,512]{1,0:T(1,128)} %param.13) | copy-start | bytes 6148
  12.9 58.3 %all-gather.9.cloned.1.call-start = ((), (), s32[]{:S(2)}) async-start(), calls=%async_computation.1 | async-start | bytes 1310720 | tf_op jit(solution)/shard_map/all_gather | solution.py:96
  17.2 296.0 %reduce-scatter.2.cloned.1.call-start = ((), (), s32[]{:S(2)}) async-start(), calls=%async_computation.3 | async-start | bytes 2621440 | tf_op jit(solution)/shard_map/reduce_scatter | solution.py:139
  73.4 3.7 %copy-start.3 = (bf16[128,1024]{1,0:T(8,128)(2,1)}, bf16[128,1024]{1,0:T(8,128)(2,1)S(1)}, u32[]{:S(2)}) copy-start(bf16[128,1024]{1,0:T(8,128)(2,1)S(1)} %fusion.6) | copy-start | bytes 786436
  77.6 0.7 copy-start.1
  78.4 7.9 %collective-permute-start = (bf16[128,1024]{1,0:T(8,128)(2,1)}, bf16[128,1024]{1,0:T(8,128)(2,1)S(1)}, u32[]{:S(2)}, u32[]{:S(2)}) collective-permute-start(bf16[128,1024]{1,0:T(8,128)(2,1)} %get-tuple-element.429), channel_id=1, source_target_pairs={{0,4},{4,8},{8,12},{12,16},{16,20},{20,24},{24,28},{28,0},{1,5},{5... | collective-permute-start | bytes 786440 | tf_op jit(solution)/shard_map/while/body/eval_jaxpr/ppermute | solution.py:13
  87.6 7.8 %collective-permute-start = (bf16[128,1024]{1,0:T(8,128)(2,1)}, bf16[128,1024]{1,0:T(8,128)(2,1)S(1)}, u32[]{:S(2)}, u32[]{:S(2)}) collective-permute-start(bf16[128,1024]{1,0:T(8,128)(2,1)} %get-tuple-element.429), channel_id=1, source_target_pairs={{0,4},{4,8},{8,12},{12,16},{16,20},{20,24},{24,28},{28,0},{1,5},{5... | collective-permute-start | bytes 786440 | tf_op jit(solution)/shard_map/while/body/eval_jaxpr/ppermute | solution.py:13
  96.7 7.8 %collective-permute-start = (bf16[128,1024]{1,0:T(8,128)(2,1)}, bf16[128,1024]{1,0:T(8,128)(2,1)S(1)}, u32[]{:S(2)}, u32[]{:S(2)}) collective-permute-start(bf16[128,1024]{1,0:T(8,128)(2,1)} %get-tuple-element.429), channel_id=1, source_target_pairs={{0,4},{4,8},{8,12},{12,16},{16,20},{20,24},{24,28},{28,0},{1,5},{5... | collective-permute-start | bytes 786440 | tf_op jit(solution)/shard_map/while/body/eval_jaxpr/ppermute | solution.py:13
  105.8 7.8 %collective-permute-start = (bf16[128,1024]{1,0:T(8,128)(2,1)}, bf16[128,1024]{1,0:T(8,128)(2,1)S(1)}, u32[]{:S(2)}, u32[]{:S(2)}) collective-permute-start(bf16[128,1024]{1,0:T(8,128)(2,1)} %get-tuple-element.429), channel_id=1, source_target_pairs={{0,4},{4,8},{8,12},{12,16},{16,20},{20,24},{24,28},{28,0},{1,5},{5... | collective-permute-start | bytes 786440 | tf_op jit(solution)/shard_map/while/body/eval_jaxpr/ppermute | solution.py:13
  114.9 7.8 %collective-permute-start = (bf16[128,1024]{1,0:T(8,128)(2,1)}, bf16[128,1024]{1,0:T(8,128)(2,1)S(1)}, u32[]{:S(2)}, u32[]{:S(2)}) collective-permute-start(bf16[128,1024]{1,0:T(8,128)(2,1)} %get-tuple-element.429), channel_id=1, source_target_pairs={{0,4},{4,8},{8,12},{12,16},{16,20},{20,24},{24,28},{28,0},{1,5},{5... | collective-permute-start | bytes 786440 | tf_op jit(solution)/shard_map/while/body/eval_jaxpr/ppermute | solution.py:13
  124.0 7.8 %collective-permute-start = (bf16[128,1024]{1,0:T(8,128)(2,1)}, bf16[128,1024]{1,0:T(8,128)(2,1)S(1)}, u32[]{:S(2)}, u32[]{:S(2)}) collective-permute-start(bf16[128,1024]{1,0:T(8,128)(2,1)} %get-tuple-element.429), channel_id=1, source_target_pairs={{0,4},{4,8},{8,12},{12,16},{16,20},{20,24},{24,28},{28,0},{1,5},{5... | collective-permute-start | bytes 786440 | tf_op jit(solution)/shard_map/while/body/eval_jaxpr/ppermute | solution.py:13
  133.1 7.8 %collective-permute-start = (bf16[128,1024]{1,0:T(8,128)(2,1)}, bf16[128,1024]{1,0:T(8,128)(2,1)S(1)}, u32[]{:S(2)}, u32[]{:S(2)}) collective-permute-start(bf16[128,1024]{1,0:T(8,128)(2,1)} %get-tuple-element.429), channel_id=1, source_target_pairs={{0,4},{4,8},{8,12},{12,16},{16,20},{20,24},{24,28},{28,0},{1,5},{5... | collective-permute-start | bytes 786440 | tf_op jit(solution)/shard_map/while/body/eval_jaxpr/ppermute | solution.py:13
  142.3 25.7 %copy-start.2 = (f32[512,128]{0,1:T(8,128)S(1)}, f32[512,128]{0,1:T(8,128)}, u32[]{:S(2)}) copy-start(f32[512,128]{0,1:T(8,128)} %copy-done.1) | copy-start | bytes 786436
  170.6 7.8 %collective-permute-start.1 = (bf16[128,1024]{1,0:T(8,128)(2,1)}, bf16[128,1024]{1,0:T(8,128)(2,1)S(1)}, u32[]{:S(2)}, u32[]{:S(2)}) collective-permute-start(bf16[128,1024]{1,0:T(8,128)(2,1)} %get-tuple-element.478), channel_id=1, source_target_pairs={{0,4},{4,8},{8,12},{12,16},{16,20},{20,24},{24,28},{28,0},{1,5},{5... | collective-permute-start | bytes 786440 | tf_op jit(solution)/shard_map/while/body/eval_jaxpr/ppermute | solution.py:13
  170.6 13.5 %collective-permute-start.2 = (f32[128,1024]{1,0:T(8,128)}, f32[128,1024]{1,0:T(8,128)}, u32[]{:S(2)}, u32[]{:S(2)}) collective-permute-start(f32[128,1024]{1,0:T(8,128)} %get-tuple-element.479), channel_id=1, source_target_pairs={{0,4},{4,8},{8,12},{12,16},{16,20},{20,24},{24,28},{28,0},{1,5},{5... | collective-permute-start | bytes 1572872 | tf_op jit(solution)/shard_map/while/body/eval_jaxpr/ppermute | solution.py:13
  186.3 7.8 %collective-permute-start.1 = (bf16[128,1024]{1,0:T(8,128)(2,1)}, bf16[128,1024]{1,0:T(8,128)(2,1)S(1)}, u32[]{:S(2)}, u32[]{:S(2)}) collective-permute-start(bf16[128,1024]{1,0:T(8,128)(2,1)} %get-tuple-element.478), channel_id=1, source_target_pairs={{0,4},{4,8},{8,12},{12,16},{16,20},{20,24},{24,28},{28,0},{1,5},{5... | collective-permute-start | bytes 786440 | tf_op jit(solution)/shard_map/while/body/eval_jaxpr/ppermute | solution.py:13
  186.3 13.5 %collective-permute-start.2 = (f32[128,1024]{1,0:T(8,128)}, f32[128,1024]{1,0:T(8,128)}, u32[]{:S(2)}, u32[]{:S(2)}) collective-permute-start(f32[128,1024]{1,0:T(8,128)} %get-tuple-element.479), channel_id=1, source_target_pairs={{0,4},{4,8},{8,12},{12,16},{16,20},{20,24},{24,28},{28,0},{1,5},{5... | collective-permute-start | bytes 1572872 | tf_op jit(solution)/shard_map/while/body/eval_jaxpr/ppermute | solution.py:13
  202.0 7.8 %collective-permute-start.1 = (bf16[128,1024]{1,0:T(8,128)(2,1)}, bf16[128,1024]{1,0:T(8,128)(2,1)S(1)}, u32[]{:S(2)}, u32[]{:S(2)}) collective-permute-start(bf16[128,1024]{1,0:T(8,128)(2,1)} %get-tuple-element.478), channel_id=1, source_target_pairs={{0,4},{4,8},{8,12},{12,16},{16,20},{20,24},{24,28},{28,0},{1,5},{5... | collective-permute-start | bytes 786440 | tf_op jit(solution)/shard_map/while/body/eval_jaxpr/ppermute | solution.py:13
  202.0 13.5 %collective-permute-start.2 = (f32[128,1024]{1,0:T(8,128)}, f32[128,1024]{1,0:T(8,128)}, u32[]{:S(2)}, u32[]{:S(2)}) collective-permute-start(f32[128,1024]{1,0:T(8,128)} %get-tuple-element.479), channel_id=1, source_target_pairs={{0,4},{4,8},{8,12},{12,16},{16,20},{20,24},{24,28},{28,0},{1,5},{5... | collective-permute-start | bytes 1572872 | tf_op jit(solution)/shard_map/while/body/eval_jaxpr/ppermute | solution.py:13
  217.7 7.8 %collective-permute-start.1 = (bf16[128,1024]{1,0:T(8,128)(2,1)}, bf16[128,1024]{1,0:T(8,128)(2,1)S(1)}, u32[]{:S(2)}, u32[]{:S(2)}) collective-permute-start(bf16[128,1024]{1,0:T(8,128)(2,1)} %get-tuple-element.478), channel_id=1, source_target_pairs={{0,4},{4,8},{8,12},{12,16},{16,20},{20,24},{24,28},{28,0},{1,5},{5... | collective-permute-start | bytes 786440 | tf_op jit(solution)/shard_map/while/body/eval_jaxpr/ppermute | solution.py:13
  217.7 13.5 %collective-permute-start.2 = (f32[128,1024]{1,0:T(8,128)}, f32[128,1024]{1,0:T(8,128)}, u32[]{:S(2)}, u32[]{:S(2)}) collective-permute-start(f32[128,1024]{1,0:T(8,128)} %get-tuple-element.479), channel_id=1, source_target_pairs={{0,4},{4,8},{8,12},{12,16},{16,20},{20,24},{24,28},{28,0},{1,5},{5... | collective-permute-start | bytes 1572872 | tf_op jit(solution)/shard_map/while/body/eval_jaxpr/ppermute | solution.py:13
  233.4 7.8 %collective-permute-start.1 = (bf16[128,1024]{1,0:T(8,128)(2,1)}, bf16[128,1024]{1,0:T(8,128)(2,1)S(1)}, u32[]{:S(2)}, u32[]{:S(2)}) collective-permute-start(bf16[128,1024]{1,0:T(8,128)(2,1)} %get-tuple-element.478), channel_id=1, source_target_pairs={{0,4},{4,8},{8,12},{12,16},{16,20},{20,24},{24,28},{28,0},{1,5},{5... | collective-permute-start | bytes 786440 | tf_op jit(solution)/shard_map/while/body/eval_jaxpr/ppermute | solution.py:13
  233.4 13.5 %collective-permute-start.2 = (f32[128,1024]{1,0:T(8,128)}, f32[128,1024]{1,0:T(8,128)}, u32[]{:S(2)}, u32[]{:S(2)}) collective-permute-start(f32[128,1024]{1,0:T(8,128)} %get-tuple-element.479), channel_id=1, source_target_pairs={{0,4},{4,8},{8,12},{12,16},{16,20},{20,24},{24,28},{28,0},{1,5},{5... | collective-permute-start | bytes 1572872 | tf_op jit(solution)/shard_map/while/body/eval_jaxpr/ppermute | solution.py:13
  249.1 7.8 %collective-permute-start.1 = (bf16[128,1024]{1,0:T(8,128)(2,1)}, bf16[128,1024]{1,0:T(8,128)(2,1)S(1)}, u32[]{:S(2)}, u32[]{:S(2)}) collective-permute-start(bf16[128,1024]{1,0:T(8,128)(2,1)} %get-tuple-element.478), channel_id=1, source_target_pairs={{0,4},{4,8},{8,12},{12,16},{16,20},{20,24},{24,28},{28,0},{1,5},{5... | collective-permute-start | bytes 786440 | tf_op jit(solution)/shard_map/while/body/eval_jaxpr/ppermute | solution.py:13
  249.1 13.5 %collective-permute-start.2 = (f32[128,1024]{1,0:T(8,128)}, f32[128,1024]{1,0:T(8,128)}, u32[]{:S(2)}, u32[]{:S(2)}) collective-permute-start(f32[128,1024]{1,0:T(8,128)} %get-tuple-element.479), channel_id=1, source_target_pairs={{0,4},{4,8},{8,12},{12,16},{16,20},{20,24},{24,28},{28,0},{1,5},{5... | collective-permute-start | bytes 1572872 | tf_op jit(solution)/shard_map/while/body/eval_jaxpr/ppermute | solution.py:13
  264.8 7.8 %collective-permute-start.1 = (bf16[128,1024]{1,0:T(8,128)(2,1)}, bf16[128,1024]{1,0:T(8,128)(2,1)S(1)}, u32[]{:S(2)}, u32[]{:S(2)}) collective-permute-start(bf16[128,1024]{1,0:T(8,128)(2,1)} %get-tuple-element.478), channel_id=1, source_target_pairs={{0,4},{4,8},{8,12},{12,16},{16,20},{20,24},{24,28},{28,0},{1,5},{5... | collective-permute-start | bytes 786440 | tf_op jit(solution)/shard_map/while/body/eval_jaxpr/ppermute | solution.py:13
  264.8 13.5 %collective-permute-start.2 = (f32[128,1024]{1,0:T(8,128)}, f32[128,1024]{1,0:T(8,128)}, u32[]{:S(2)}, u32[]{:S(2)}) collective-permute-start(f32[128,1024]{1,0:T(8,128)} %get-tuple-element.479), channel_id=1, source_target_pairs={{0,4},{4,8},{8,12},{12,16},{16,20},{20,24},{24,28},{28,0},{1,5},{5... | collective-permute-start | bytes 1572872 | tf_op jit(solution)/shard_map/while/body/eval_jaxpr/ppermute | solution.py:13
  280.5 1.0 copy-start.4
  281.6 10.4 %collective-permute-start.3 = (f32[128,1024]{1,0:T(8,128)S(1)}, f32[128,1024]{1,0:T(8,128)S(1)}, u32[]{:S(2)}, u32[]{:S(2)}) collective-permute-start(f32[128,1024]{1,0:T(8,128)S(1)} %copy-done.4), channel_id=1, source_target_pairs={{0,4},{4,8},{8,12},{12,16},{16,20},{20,24},{24,28},{28,0},{1,5},{5... | collective-permute-start | bytes 1572872 | tf_op jit(solution)/shard_map/ppermute | solution.py:13
Sparse Core Ops, SparseCore 0:
  13.0 29.1 all-gather.10
  44.7 26.4 all-gather.8
  280.7 32.4 reduce-scatter.1
where the time goes:
time: 324 us; the launch traced here: 323 us
  waiting for transfers between devices  198 us (61%)
  matrix products  58.5 us (18%)
  blocking collectives  23.3 us (7%)
  local copies, waits for them, and re-layouts  14.6 us (5%)
  other arithmetic  14 us (4%)
  between operations  13.8 us (4%)
    ppermute x22, waiting for transfers between devices, shifted(): return lax.ppermute(value, axis, pairs)  128 us
    all_gather x1, waiting for transfers between devices, body(): lax.all_gather(key_part, 'tensor', axis=1, tiled=True)  27.4 us
    dot_general x8, matrix products, contributions(): jnp.dot(weights, key_block, preferred_element_type=jnp.float32)  25.9 us
    all_gather x1, waiting for transfers between devices, body(): lax.all_gather(query_part, 'tensor', axis=1, tiled=True)  25 us
    all_gather x3, blocking collectives, combined_all(): gathered = jax.tree.map(lambda a: lax.all_gather(a, axis), part)  23.3 us
    reduce_scatter x1, waiting for transfers between devices, body(): lax.psum_scatter(grad_q, 'tensor', scatter_dimension=0, tiled=True)  18.1 us
    dot_general x8, matrix products, contributions(): lax.dot_general(weights, queries_unit, (((0,), (0,)), ((), ())), preferre...  17.2 us
    while x21, local copies, waits for them, and re-layouts  9.87 us
  transfers between devices with their start and end apart: 25, of which 25 were waited for; matrix products, arithmetic and copies ran while one was open for 13% of the time, Pallas kernels for 0%

commit v1 on v0

v1 whole, which is shorter than its diff:
```python
import functools

import jax
import jax.numpy as jnp
from jax import lax
from jax.experimental import pallas as pl
from jax.experimental.pallas import tpu as pltpu
from jax.sharding import PartitionSpec as P

SCALE = 100.0
EPSILON = 1e-06
MESH = pl.DeviceIdType.MESH
HALVES = 2


def kernel(
    chips, groups, q_ref, k_ref, pos_ref, loss_ref, gq_ref, gk_ref,
    kraw, kunit, kall, qraw, qhat, scores, weights, stats,
    sib_out, sib_in, ring_out, ring_in, gq_out, gq_in,
    kx_send, kx_recv, qx_send, qx_recv, ring_send, fwd_send, k_recv,
    st_send, st_recv, sb_send, sb_recv, rg_send, rg_recv, gq_send, gq_recv,
):
    rows, feats = q_ref.shape
    part = rows // groups
    half = part // HALVES
    me = lax.axis_index("dp")
    t = lax.axis_index("tensor")
    chip, core = me // 2, me % 2
    other = 1 - core
    sibling = chip * 2 + other
    right = lax.rem(chip + 1, chips) * 2 + core
    left = lax.rem(chip + chips - 1, chips) * 2 + core

    def peer(i):
        return lax.rem(t + i, groups)

    def remote(src, dst, send, recv, device):
        return pltpu.make_async_remote_copy(
            src_ref=src, dst_ref=dst, send_sem=send, recv_sem=recv,
            device_id=device, device_id_type=MESH,
        )

    barrier = pltpu.get_barrier_semaphore()
    for i in range(1, groups):
        pl.semaphore_signal(barrier, inc=1, device_id=(me, peer(i)), device_id_type=MESH)
    for device in (sibling, right, left):
        pl.semaphore_signal(barrier, inc=1, device_id=(device, t), device_id_type=MESH)
    pl.semaphore_wait(barrier, groups + 2)

    def kx_copy(i):
        rows_of = pl.ds(pl.multiple_of(peer(i) * part, part), part)
        return remote(k_ref.at[rows_of], kraw.at[t], kx_send.at[i], kx_recv.at[t], (me, peer(i)))

    def kx_from(i):
        slot = kraw.at[peer(i)]
        return remote(slot, slot, kx_send.at[i], kx_recv.at[peer(i)], (me, peer(i)))

    def qx_copy(i):
        return remote(q_ref, qraw.at[t], qx_send.at[i], qx_recv.at[t], (me, peer(i)))

    def qx_from(i):
        slot = qraw.at[peer(i)]
        return remote(slot, slot, qx_send.at[i], qx_recv.at[peer(i)], (me, peer(i)))

    for i in range(1, groups):
        kx_copy(i).start()
    kraw[t] = k_ref[pl.ds(pl.multiple_of(t * part, part), part)]
    qraw[t] = q_ref[...]
    for i in range(1, groups):
        kx_from(i).wait_recv()

    def inverse_magnitude(blocks):
        total = blocks[0] * blocks[0]
        for block in blocks[1:]:
            total = total + block * block
        return lax.rsqrt(jnp.sum(total, axis=1, keepdims=True) + EPSILON)

    entries = [kraw[s].astype(jnp.float32) for s in range(groups)]
    k_inverse = inverse_magnitude(entries)
    for s in range(groups):
        unit = entries[s] * k_inverse
        kunit[:, s * feats : (s + 1) * feats] = unit
        kall[me, :, s * feats : (s + 1) * feats] = unit.astype(jnp.bfloat16)

    def source(s):
        return lax.rem(chip + chips - s, chips) * 2

    def ring_copy(s, h):
        slot = kall.at[source(s) + core, pl.ds(h * half, half)]
        return remote(slot, slot, ring_send.at[s, h], k_recv.at[source(s) + core, h], (right, t))

    def fwd_copy(s, h):
        slot = kall.at[source(s) + core, pl.ds(h * half, half)]
        return remote(slot, slot, fwd_send.at[s, h], k_recv.at[source(s) + core, h], (sibling, t))

    def k_from(index, h):
        slot = kall.at[index, pl.ds(h * half, half)]
        return remote(slot, slot, ring_send.at[0, h], k_recv.at[index, h], (right, t))

    def forward(s):
        for h in range(HALVES):
            if s > 0:
                k_from(source(s) + core, h).wait_recv()
            if s < chips - 1:
                ring_copy(s, h).start()
            fwd_copy(s, h).start()

    forward(0)
    for i in range(1, groups):
        qx_copy(i).start()
    for s in range(1, chips - 1):
        forward(s)

    for i in range(1, groups):
        qx_from(i).wait_recv()

    def normalize_rows(p, carried):
        span = pl.ds(pl.multiple_of(p * part, part), part)
        blocks = [qraw[s, span].astype(jnp.float32) for s in range(groups)]
        inverse = inverse_magnitude(blocks)
        for s in range(groups):
            qhat[span, s * feats : (s + 1) * feats] = (blocks[s] * inverse).astype(jnp.bfloat16)
        return carried

    lax.fori_loop(0, groups, normalize_rows, 0)

    def score(index):
        block = SCALE * lax.dot_general(
            kall[index], qhat[...], (((1,), (1,)), ((), ())), preferred_element_type=jnp.float32
        )
        scores[index] = block
        return block

    def fold(index, state):
        row_max, row_sum = state
        block = score(index)
        new_max = jnp.maximum(row_max, jnp.max(block, axis=0, keepdims=True))
        row_sum = row_sum * jnp.exp(row_max - new_max) + jnp.sum(
            jnp.exp(block - new_max), axis=0, keepdims=True
        )
        return (new_max, row_sum)

    def positive_mask():
        key_index = lax.broadcasted_iota(jnp.int32, (part, rows), 0)
        return (key_index == pos_ref[...] - t * part).astype(jnp.float32)

    own = score(me)
    row_max = jnp.max(own, axis=0, keepdims=True)
    row_sum = jnp.sum(jnp.exp(own - row_max), axis=0, keepdims=True)
    matched = jnp.sum(own * positive_mask(), axis=0, keepdims=True)

    def from_sibling(s):
        for h in range(HALVES):
            k_from(source(s) + other, h).wait_recv()

    def fold_pair(s, state):
        state = fold(source(s) + core, state)
        from_sibling(s)
        return fold(source(s) + other, state)

    from_sibling(0)
    state = fold(source(0) + other, (row_max, row_sum))
    state = lax.fori_loop(1, chips - 1, fold_pair, state)
    forward(chips - 1)
    row_max, row_sum = fold_pair(chips - 1, state)

    stats[t, 0:1] = row_max
    stats[t, 1:2] = row_sum
    stats[t, 2:3] = matched

    def st_copy(i):
        return remote(stats.at[t], stats.at[t], st_send.at[i], st_recv.at[t], (me, peer(i)))

    def st_from(i):
        slot = stats.at[peer(i)]
        return remote(slot, slot, st_send.at[i], st_recv.at[peer(i)], (me, peer(i)))

    for i in range(1, groups):
        st_copy(i).start()
    for i in range(1, groups):
        st_from(i).wait_recv()
    best = stats[0, 0:1]
    for s in range(1, groups):
        best = jnp.maximum(best, stats[s, 0:1])
    total = jnp.zeros_like(best)
    matched = jnp.zeros_like(best)
    for s in range(groups):
        total = total + stats[s, 1:2] * jnp.exp(stats[s, 0:1] - best)
        matched = matched + stats[s, 2:3]
    log_total = best + jnp.log(total)
    loss_ref[...] = log_total - matched

    def weigh(index, carried):
        weights[index] = jnp.exp(scores[index] - log_total).astype(jnp.bfloat16)
        return carried

    lax.fori_loop(0, 2 * chips, weigh, 0)
    weights[me] = (jnp.exp(scores[me] - log_total) - positive_mask()).astype(jnp.bfloat16)

    def target(i):
        return lax.rem(chip + 2 * chips - 1 - i, chips) * 2

    def key_part(index):
        return jnp.dot(weights[index], qhat[...], preferred_element_type=jnp.float32)

    def sb_copy(i):
        return remote(sib_out.at[i], sib_in.at[i], sb_send.at[i], sb_recv.at[i], (sibling, t))

    def rg_copy(i, h):
        span = pl.ds(h * half, half)
        return remote(
            ring_out.at[i, span], ring_in.at[i, span], rg_send.at[i, h], rg_recv.at[i, h], (right, t)
        )

    def hand_over(i, carried):
        sib_out[i] = key_part(target(i) + other).astype(jnp.bfloat16)
        sb_copy(i).start()
        return carried

    def ring_first():
        value = key_part(target(0) + core)
        sb_copy(0).wait_recv()
        for h in range(HALVES):
            span = slice(h * half, (h + 1) * half)
            ring_out[0, span] = (value[span] + sib_in[0, span].astype(jnp.float32)).astype(jnp.bfloat16)
            rg_copy(0, h).start()

    def ring_next(i, carried):
        value = key_part(target(i) + core)
        sb_copy(i).wait_recv()
        for h in range(HALVES):
            span = slice(h * half, (h + 1) * half)
            both = value[span] + sib_in[i, span].astype(jnp.float32)
            rg_copy(i - 1, h).wait_recv()
            ring_out[i, span] = (both + ring_in[i - 1, span].astype(jnp.float32)).astype(jnp.bfloat16)
            rg_copy(i, h).start()
        return carried

    hand_over(0, 0)
    ring_first()
    lax.fori_loop(1, chips, hand_over, 0)

    def query_part(p):
        span = pl.ds(pl.multiple_of(p * part, part), part)
        chosen = weights[:, :, span].reshape(2 * chips * part, part)
        keys = kall[...].reshape(2 * chips * part, groups * feats)
        return lax.dot_general(
            chosen, keys, (((0,), (0,)), ((), ())), preferred_element_type=jnp.float32
        )

    def gq_copy(i):
        return remote(gq_out.at[i - 1], gq_in.at[i - 1], gq_send.at[i - 1], gq_recv.at[i - 1], (me, peer(i)))

    def query_send(i, carried):
        gq_out[i - 1] = query_part(peer(i)).astype(jnp.bfloat16)
        gq_copy(i).start()
        return carried

    lax.fori_loop(1, groups, query_send, 0)
    gq_ref[...] = query_part(t)
    lax.fori_loop(1, chips - 1, ring_next, 0)

    def unnormalized(grad, unit, inverse):
        grad = grad * SCALE
        return (grad - unit * jnp.sum(unit * grad, axis=1, keepdims=True)) * inverse

    value = gq_ref[...]
    for i in range(1, groups):
        gq_copy(i).wait_recv()
        value = value + gq_in[i - 1].astype(jnp.float32)
    own_rows = pl.ds(pl.multiple_of(t * part, part), part)
    blocks = [qraw[s, own_rows].astype(jnp.float32) for s in range(groups)]
    inverse = inverse_magnitude(blocks)
    gq_ref[...] = unnormalized(value, jnp.concatenate(blocks, axis=1) * inverse, inverse)

    value = key_part(me)
    sb_copy(chips - 1).wait_recv()
    value = value + sib_in[chips - 1].astype(jnp.float32)
    for h in range(HALVES):
        rg_copy(chips - 2, h).wait_recv()
    value = value + ring_in[chips - 2].astype(jnp.float32)
    gk_ref[...] = unnormalized(value, kunit[...], k_inverse)

    for i in range(1, groups):
        kx_copy(i).wait_send()
        qx_copy(i).wait_send()
        st_copy(i).wait_send()
        gq_copy(i).wait_send()
    for s in range(chips):
        sb_copy(s).wait_send()
        for h in range(HALVES):
            fwd_copy(s, h).wait_send()
            if s < chips - 1:
                ring_copy(s, h).wait_send()
                rg_copy(s, h).wait_send()


def body(queries, keys, projection, positives):
    dp, groups = lax.axis_size("dp"), lax.axis_size("tensor")
    chips = dp // 2
    rows = queries.shape[0]
    part = rows // groups
    feats = projection.shape[1]
    width = feats * groups
    key_feats = jnp.dot(keys, projection, preferred_element_type=jnp.float32).astype(jnp.bfloat16)
    query_feats = jnp.dot(queries, projection, preferred_element_type=jnp.float32).astype(jnp.bfloat16)
    bf16, f32 = jnp.bfloat16, jnp.float32
    vmem, dma = pltpu.VMEM, pltpu.SemaphoreType.DMA
    spec = pl.BlockSpec(memory_space=pltpu.VMEM)
    loss, grad_q, grad_k = pl.pallas_call(
        functools.partial(kernel, chips, groups),
        out_shape=(
            jax.ShapeDtypeStruct((1, rows), f32),
            jax.ShapeDtypeStruct((part, width), f32),
            jax.ShapeDtypeStruct((part, width), f32),
        ),
        in_specs=[spec] * 3,
        out_specs=(spec,) * 3,
        scratch_shapes=[
            vmem((groups, part, feats), bf16),
            vmem((part, width), f32),
            vmem((dp, part, width), bf16),
            vmem((groups, rows, feats), bf16),
            vmem((rows, width), bf16),
            vmem((dp, part, rows), f32),
            vmem((dp, part, rows), bf16),
            vmem((groups, 8, rows), f32),
            vmem((chips, part, width), bf16),
            vmem((chips, part, width), bf16),
            vmem((chips - 1, part, width), bf16),
            vmem((chips - 1, part, width), bf16),
            vmem((groups - 1, part, width), bf16),
            vmem((groups - 1, part, width), bf16),
            dma((groups,)), dma((groups,)), dma((groups,)), dma((groups,)),
            dma((chips, HALVES)), dma((chips, HALVES)), dma((dp, HALVES)),
            dma((groups,)), dma((groups,)),
            dma((chips,)), dma((chips,)),
            dma((chips, HALVES)), dma((chips, HALVES)),
            dma((groups,)), dma((groups,)),
        ],
        compiler_params=pltpu.CompilerParams(
            collective_id=0, has_side_effects=True, vmem_limit_bytes=60 * 1024 * 1024
        ),
        cost_estimate=pl.CostEstimate(
            flops=8 * rows * dp * part * width, bytes_accessed=8 * part * width * 4,
            transcendentals=2 * rows * dp * part,
        ),
    )(query_feats, key_feats, positives)
    row_start = lax.axis_index("tensor") * part
    pair_loss = lax.dynamic_slice_in_dim(loss[0], row_start, part, 0)
    return (pair_loss, grad_q, grad_k)


def solution(mesh):
    in_specs = (P("dp", None), P("dp", None), P(None, "tensor"), P("dp", None))
    out_specs = (P(("dp", "tensor")), P(("dp", "tensor"), None), P(("dp", "tensor"), None))
    return jax.shard_map(body, mesh=mesh, in_specs=in_specs, out_specs=out_specs, check_vma=False)
```

time: 324 us -> 70.7 us (0.22)
  waiting for transfers between devices: 198 us -> 0 us
  Pallas kernels: 0 us -> 56.9 us
  matrix products: 58.5 us -> 6.36 us
  blocking collectives: 23.3 us -> 0 us
  other arithmetic: 14 us -> 0 us
  between operations: 13.8 us -> 0.66 us
  local copies, waits for them, and re-layouts: 14.6 us -> 6.53 us
    ppermute x22 -> x0, waiting for transfers between devices: 128 us -> none  [shifted(): return lax.ppermute(value, axis, pairs)]
    pallas_call x0 -> x1, Pallas kernels: none -> 56.9 us  [body(): pl.pallas_call(functools.partial(kernel, chips, groups), out_shape=(jax.S...]
    all_gather x2 -> x0, waiting for transfers between devices: 52.5 us -> none  [the longest x1 27.4 us: body(): lax.all_gather(key_part, 'tensor', axis=1, tiled=True)]
    dot_general x31 -> x0, matrix products: 50.2 us -> none  [the longest x8 25.9 us: contributions(): jnp.dot(weights, key_block, preferred_element_type=jnp.float32)]
    all_gather x3 -> x0, blocking collectives: 23.3 us -> none  [combined_all(): gathered = jax.tree.map(lambda a: lax.all_gather(a, axis), part)]
    reduce_scatter x1 -> x0, waiting for transfers between devices: 18.1 us -> none  [body(): lax.psum_scatter(grad_q, 'tensor', scatter_dimension=0, tiled=True)]
    while x21 -> x0, local copies, waits for them, and re-layouts: 9.87 us -> none
    div x3 -> x0, other arithmetic: 7.05 us -> none  [the longest x2 4.08 us: unnormalize(): (grad_unit - unit_rows * jnp.sum(unit_rows * grad_unit, axis=1, keepdims=...]
  transfers between devices with their start and end apart: 25 -> 0, of which waited for: 25 -> 0; matrix products, arithmetic and copies ran while one was open for 13% -> 0% of each run, Pallas kernels for 0% -> 0%
where the time goes in v1:
time: 70.7 us; the launch traced here: 70.5 us
  Pallas kernels  56.9 us (80%)
  local copies, waits for them, and re-layouts  6.53 us (9%)
  matrix products  6.36 us (9%)
    pallas_call x1, Pallas kernels, body(): pl.pallas_call(functools.partial(kernel, chips, groups), out_shape=(jax.S...  56.9 us
    unnamed x6, local copies, waits for them, and re-layouts  5.35 us
    dot_general x1, matrix products, body(): jnp.dot(queries, projection, preferred_element_type=jnp.float32)  4.39 us
    dot_general x1, matrix products, body(): jnp.dot(keys, projection, preferred_element_type=jnp.float32)  1.97 us

profile of v1, /device:TPU:0, one launch (start us, length us, event | category | flops | bytes accessed | tf_op | source)
XLA Modules:
  0.0 70.5 jit_solution(9850350724033863149)
XLA Ops:
  0.6 0.0 copy-start
  0.6 0.0 copy-start.1
  0.7 1.6 %copy-done = bf16[4096,256]{1,0:T(8,128)(2,1)S(1)} copy-done((bf16[4096,256]{1,0:T(8,128)(2,1)S(1)}, bf16[4096,256]{1,0:T(8,128)(2,1)}, u32[]{:S(2)}) %copy-start) | copy-done | bytes 2097176
  2.2 4.4 %convolution_convert_fusion.1.q_ref = bf16[512,256]{1,0:T(8,128)(2,1)} fusion(bf16[512,4096]{1,0:T(8,128)(2,1)} %param.4, bf16[4096,256]{1,0:T(8,128)(2,1)S(1)} %copy-done), kind=kOutput, calls=%fused_computation.1 | convolution fusion | flops 1073872896 | bytes 6553600 | tf_op jit(solution)/shard_map/dot_general | solution.py:306
  6.6 0.0 copy-done.1
  6.6 2.0 %convolution_convert_fusion.k_ref = bf16[512,256]{1,0:T(8,128)(2,1)} fusion(bf16[512,4096]{1,0:T(8,128)(2,1)S(1)} %copy-done.1, bf16[4096,256]{1,0:T(8,128)(2,1)S(1)} %copy-done), kind=kOutput, calls=%fused_computation | convolution fusion | flops 1073872896 | bytes 6553600 | tf_op jit(solution)/shard_map/dot_general | solution.py:305
  8.6 56.9 %shard_map.67 = (f32[1,512]{1,0:T(1,128)}, f32[128,1024]{1,0:T(8,128)}, f32[128,1024]{1,0:T(8,128)}) custom-call(bf16[512,256]{1,0:T(8,128)(2,1)} %convolution_convert_fusion.1.q_ref, bf16[512,256]{1,0:T(8,128)(2,1)} %convolution_convert_fusion.k_ref, s32[1,512]{1,0:T(1,128)} %pos_ref.1), custom_call_target="tpu_custom_call" | custom-call | flops 4294967296 | bytes 4194304 | tf_op jit(solution)/shard_map/pallas_call | solution.py:310
  65.5 1.2 %dynamic-slice_bitcast_fusion = f32[128]{0:T(128)} fusion(f32[1,512]{1,0:T(1,128)} %get-tuple-element.6, s32[]{:T(128)S(6)} %select_n.3), kind=kLoop, calls=%fused_computation.2 | loop fusion | bytes 1028 | tf_op jit(solution)/shard_map/dynamic_slice | solution.py:350
  66.7 1.9 %copy.9 = f32[128,1024]{1,0:T(8,128)} copy(f32[128,1024]{1,0:T(8,128)} %get-tuple-element.13) | data formatting | bytes 1048576
  68.6 1.9 %copy.10 = f32[128,1024]{1,0:T(8,128)} copy(f32[128,1024]{1,0:T(8,128)} %get-tuple-element.14) | data formatting | bytes 1048576
Async XLA Ops:
  0.6 1.6 %copy-start = (bf16[4096,256]{1,0:T(8,128)(2,1)S(1)}, bf16[4096,256]{1,0:T(8,128)(2,1)}, u32[]{:S(2)}) copy-start(bf16[4096,256]{1,0:T(8,128)(2,1)} %param.6) | copy-start | bytes 6291460
  0.6 6.0 %copy-start.1 = (bf16[512,4096]{1,0:T(8,128)(2,1)S(1)}, bf16[512,4096]{1,0:T(8,128)(2,1)}, u32[]{:S(2)}) copy-start(bf16[512,4096]{1,0:T(8,128)(2,1)} %param.5) | copy-start | bytes 12582916

commit v2 on v1

--- a/solution.py
+++ b/solution.py
@@ -11,16 +11,19 @@
 EPSILON = 1e-06
 MESH = pl.DeviceIdType.MESH
 HALVES = 2
+DEPTH = 512
+STAGE_BYTES = 4 * 1024 * 1024
 
 
 def kernel(
-    chips, groups, q_ref, k_ref, pos_ref, loss_ref, gq_ref, gk_ref,
-    kraw, kunit, kall, qraw, qhat, scores, weights, stats,
-    sib_out, sib_in, ring_out, ring_in, gq_out, gq_in,
+    chips, groups, q_hbm, k_hbm, w_hbm, pos_ref, loss_ref, gq_ref, gk_ref,
+    stage, w_in, kfeat, kraw, kall, qraw, qhat, scores, weights, stats,
+    sib_out, sib_in, ring_in, gq_out, gq_in, stage_sem, w_sem,
     kx_send, kx_recv, qx_send, qx_recv, ring_send, fwd_send, k_recv,
     st_send, st_recv, sb_send, sb_recv, rg_send, rg_recv, gq_send, gq_recv,
 ):
-    rows, feats = q_ref.shape
+    rows, feats = kfeat.shape
+    slots, steps = stage.shape[0], w_in.shape[0] // DEPTH
     part = rows // groups
     half = part // HALVES
     me = lax.axis_index("dp")
@@ -45,18 +48,52 @@
         pl.semaphore_signal(barrier, inc=1, device_id=(me, peer(i)), device_id_type=MESH)
     for device in (sibling, right, left):
         pl.semaphore_signal(barrier, inc=1, device_id=(device, t), device_id_type=MESH)
+
+    def w_copy(c):
+        span = pl.ds(c * DEPTH, DEPTH)
+        return pltpu.make_async_copy(w_hbm.at[span], w_in.at[span], w_sem.at[c])
+
+    def stage_copy(c):
+        source_ref = k_hbm if c < steps else q_hbm
+        span = pl.ds((c % steps) * DEPTH, DEPTH)
+        return pltpu.make_async_copy(
+            source_ref.at[:, span], stage.at[c % slots], stage_sem.at[c % slots]
+        )
+
+    for c in range(max(steps, slots)):
+        if c < steps:
+            w_copy(c).start()
+        if c < slots:
+            stage_copy(c).start()
+
+    def project(first):
+        total = None
+        for c in range(steps):
+            if first == 0:
+                w_copy(c).wait()
+            stage_copy(first + c).wait()
+            term = jnp.dot(
+                stage[(first + c) % slots], w_in[c * DEPTH : (c + 1) * DEPTH],
+                preferred_element_type=jnp.float32,
+            )
+            total = term if total is None else total + term
+            if first + c + slots < 2 * steps:
+                stage_copy(first + c + slots).start()
+        return total.astype(jnp.bfloat16)
+
+    kfeat[...] = project(0)
     pl.semaphore_wait(barrier, groups + 2)
 
     def kx_copy(i):
         rows_of = pl.ds(pl.multiple_of(peer(i) * part, part), part)
-        return remote(k_ref.at[rows_of], kraw.at[t], kx_send.at[i], kx_recv.at[t], (me, peer(i)))
+        return remote(kfeat.at[rows_of], kraw.at[t], kx_send.at[i], kx_recv.at[t], (me, peer(i)))
 
     def kx_from(i):
         slot = kraw.at[peer(i)]
         return remote(slot, slot, kx_send.at[i], kx_recv.at[peer(i)], (me, peer(i)))
 
     def qx_copy(i):
-        return remote(q_ref, qraw.at[t], qx_send.at[i], qx_recv.at[t], (me, peer(i)))
+        return remote(qraw.at[t], qraw.at[t], qx_send.at[i], qx_recv.at[t], (me, peer(i)))
 
     def qx_from(i):
         slot = qraw.at[peer(i)]
@@ -64,8 +101,8 @@
 
     for i in range(1, groups):
         kx_copy(i).start()
-    kraw[t] = k_ref[pl.ds(pl.multiple_of(t * part, part), part)]
-    qraw[t] = q_ref[...]
+    kraw[t] = kfeat[pl.ds(pl.multiple_of(t * part, part), part)]
+    qraw[t] = project(steps)
     for i in range(1, groups):
         kx_from(i).wait_recv()
 
@@ -78,9 +115,9 @@
     entries = [kraw[s].astype(jnp.float32) for s in range(groups)]
     k_inverse = inverse_magnitude(entries)
     for s in range(groups):
-        unit = entries[s] * k_inverse
-        kunit[:, s * feats : (s + 1) * feats] = unit
-        kall[me, :, s * feats : (s + 1) * feats] = unit.astype(jnp.bfloat16)
+        kall[me, :, s * feats : (s + 1) * feats] = (entries[s] * k_inverse).astype(
+            jnp.bfloat16
+        )
 
     def source(s):
         return lax.rem(chip + chips - s, chips) * 2
@@ -209,7 +246,7 @@
     def rg_copy(i, h):
         span = pl.ds(h * half, half)
         return remote(
-            ring_out.at[i, span], ring_in.at[i, span], rg_send.at[i, h], rg_recv.at[i, h], (right, t)
+            sib_in.at[i, span], ring_in.at[i, span], rg_send.at[i, h], rg_recv.at[i, h], (right, t)
         )
 
     def hand_over(i, carried):
@@ -222,7 +259,7 @@
         sb_copy(0).wait_recv()
         for h in range(HALVES):
             span = slice(h * half, (h + 1) * half)
-            ring_out[0, span] = (value[span] + sib_in[0, span].astype(jnp.float32)).astype(jnp.bfloat16)
+            sib_in[0, span] = (value[span] + sib_in[0, span].astype(jnp.float32)).astype(jnp.bfloat16)
             rg_copy(0, h).start()
 
     def ring_next(i, carried):
@@ -232,7 +269,7 @@
             span = slice(h * half, (h + 1) * half)
             both = value[span] + sib_in[i, span].astype(jnp.float32)
             rg_copy(i - 1, h).wait_recv()
-            ring_out[i, span] = (both + ring_in[i - 1, span].astype(jnp.float32)).astype(jnp.bfloat16)
+            sib_in[i, span] = (both + ring_in[i - 1, span].astype(jnp.float32)).astype(jnp.bfloat16)
             rg_copy(i, h).start()
         return carried
 
@@ -279,7 +316,9 @@
     for h in range(HALVES):
         rg_copy(chips - 2, h).wait_recv()
     value = value + ring_in[chips - 2].astype(jnp.float32)
-    gk_ref[...] = unnormalized(value, kunit[...], k_inverse)
+    blocks = [kraw[s].astype(jnp.float32) for s in range(groups)]
+    inverse = inverse_magnitude(blocks)
+    gk_ref[...] = unnormalized(value, jnp.concatenate(blocks, axis=1) * inverse, inverse)
 
     for i in range(1, groups):
         kx_copy(i).wait_send()
@@ -302,8 +341,8 @@
     part = rows // groups
     feats = projection.shape[1]
     width = feats * groups
-    key_feats = jnp.dot(keys, projection, preferred_element_type=jnp.float32).astype(jnp.bfloat16)
-    query_feats = jnp.dot(queries, projection, preferred_element_type=jnp.float32).astype(jnp.bfloat16)
+    embed = queries.shape[1]
+    slots = min(STAGE_BYTES // (rows * DEPTH * 2), embed // DEPTH)
     bf16, f32 = jnp.bfloat16, jnp.float32
     vmem, dma = pltpu.VMEM, pltpu.SemaphoreType.DMA
     spec = pl.BlockSpec(memory_space=pltpu.VMEM)
@@ -314,11 +353,13 @@
             jax.ShapeDtypeStruct((part, width), f32),
             jax.ShapeDtypeStruct((part, width), f32),
         ),
-        in_specs=[spec] * 3,
+        in_specs=[pl.BlockSpec(memory_space=pl.ANY)] * 3 + [spec],
         out_specs=(spec,) * 3,
         scratch_shapes=[
+            vmem((slots, rows, DEPTH), bf16),
+            vmem((embed, feats), bf16),
+            vmem((rows, feats), bf16),
             vmem((groups, part, feats), bf16),
-            vmem((part, width), f32),
             vmem((dp, part, width), bf16),
             vmem((groups, rows, feats), bf16),
             vmem((rows, width), bf16),
@@ -328,9 +369,9 @@
             vmem((chips, part, width), bf16),
             vmem((chips, part, width), bf16),
             vmem((chips - 1, part, width), bf16),
-            vmem((chips - 1, part, width), bf16),
             vmem((groups - 1, part, width), bf16),
             vmem((groups - 1, part, width), bf16),
+            dma((slots,)), dma((embed // DEPTH,)),
             dma((groups,)), dma((groups,)), dma((groups,)), dma((groups,)),
             dma((chips, HALVES)), dma((chips, HALVES)), dma((dp, HALVES)),
             dma((groups,)), dma((groups,)),
@@ -339,13 +380,14 @@
             dma((groups,)), dma((groups,)),
         ],
         compiler_params=pltpu.CompilerParams(
-            collective_id=0, has_side_effects=True, vmem_limit_bytes=60 * 1024 * 1024
+            collective_id=0, has_side_effects=True, vmem_limit_bytes=62 * 1024 * 1024
         ),
         cost_estimate=pl.CostEstimate(
-            flops=8 * rows * dp * part * width, bytes_accessed=8 * part * width * 4,
+            flops=8 * rows * dp * part * width + 4 * rows * embed * feats,
+            bytes_accessed=(4 * rows + 2 * feats) * embed + 8 * part * width,
             transcendentals=2 * rows * dp * part,
         ),
-    )(query_feats, key_feats, positives)
+    )(queries, keys, projection, positives)
     row_start = lax.axis_index("tensor") * part
     pair_loss = lax.dynamic_slice_in_dim(loss[0], row_start, part, 0)
     return (pair_loss, grad_q, grad_k)

time: 70.7 us -> 64.9 us (0.918)
  matrix products: 6.36 us -> 0 us
  Pallas kernels: 56.9 us -> 59.1 us
  local copies, waits for them, and re-layouts: 6.53 us -> 4.89 us
    dot_general x2 -> x0, matrix products: 6.36 us -> none  [the longest x1 4.39 us: body(): jnp.dot(queries, projection, preferred_element_type=jnp.float32)]
    pallas_call x1, Pallas kernels: 56.9 us -> 59.1 us  [body(): pl.pallas_call(functools.partial(kernel, chips, groups), out_shape=(jax.S...]
    unnamed x6 -> x2, local copies, waits for them, and re-layouts: 5.35 us -> 3.77 us
where the time goes in v2:
time: 64.9 us; the launch traced here: 64.6 us
  Pallas kernels  59.1 us (91%)
  local copies, waits for them, and re-layouts  4.89 us (8%)
    pallas_call x1, Pallas kernels, body(): pl.pallas_call(functools.partial(kernel, chips, groups), out_shape=(jax.S...  59.1 us
    unnamed x2, local copies, waits for them, and re-layouts  3.77 us

profile of v2, /device:TPU:0, one launch (start us, length us, event | category | flops | bytes accessed | tf_op | source)
XLA Modules:
  0.0 64.6 jit_solution(5780071166841013846)
XLA Ops:
  0.6 59.1 %shard_map.67 = (f32[1,512]{1,0:T(1,128)}, f32[128,1024]{1,0:T(8,128)}, f32[128,1024]{1,0:T(8,128)}) custom-call(bf16[512,4096]{1,0:T(8,128)(2,1)} %q_hbm.1, bf16[512,4096]{1,0:T(8,128)(2,1)} %k_hbm.1, bf16[4096,256]{1,0:T(8,128)(2,1)} %w_hbm.1, s32[1,512]{1,0:T(1,128)} %pos_ref.1), custom_call_target="tpu_custom_call" | custom-call | flops 6442450944 | bytes 11534336 | tf_op jit(solution)/shard_map/pallas_call | solution.py:349
  59.7 1.1 %dynamic-slice_bitcast_fusion = f32[128]{0:T(128)} fusion(f32[1,512]{1,0:T(1,128)} %get-tuple-element.6, s32[]{:T(128)S(6)} %select_n.3), kind=kLoop, calls=%fused_computation | loop fusion | bytes 1028 | tf_op jit(solution)/shard_map/dynamic_slice | solution.py:392
  60.9 1.9 %copy.9 = f32[128,1024]{1,0:T(8,128)} copy(f32[128,1024]{1,0:T(8,128)} %get-tuple-element.13) | data formatting | bytes 1048576
  62.8 1.9 %copy.10 = f32[128,1024]{1,0:T(8,128)} copy(f32[128,1024]{1,0:T(8,128)} %get-tuple-element.14) | data formatting | bytes 1048576

commit v3 on v2

--- a/solution.py
+++ b/solution.py
@@ -231,9 +231,6 @@
         weights[index] = jnp.exp(scores[index] - log_total).astype(jnp.bfloat16)
         return carried
 
-    lax.fori_loop(0, 2 * chips, weigh, 0)
-    weights[me] = (jnp.exp(scores[me] - log_total) - positive_mask()).astype(jnp.bfloat16)
-
     def target(i):
         return lax.rem(chip + 2 * chips - 1 - i, chips) * 2
 
@@ -273,9 +270,17 @@
             rg_copy(i, h).start()
         return carried
 
-    hand_over(0, 0)
+    def weigh_pair(i, carried):
+        weigh(target(i) + other, 0)
+        hand_over(i, 0)
+        return weigh(target(i) + core, carried)
+
+    weigh_pair(0, 0)
     ring_first()
-    lax.fori_loop(1, chips, hand_over, 0)
+    lax.fori_loop(1, chips - 1, weigh_pair, 0)
+    weigh(sibling, 0)
+    hand_over(chips - 1, 0)
+    weights[me] = (jnp.exp(scores[me] - log_total) - positive_mask()).astype(jnp.bfloat16)
 
     def query_part(p):
         span = pl.ds(pl.multiple_of(p * part, part), part)
@@ -293,9 +298,11 @@
         gq_copy(i).start()
         return carried
 
-    lax.fori_loop(1, groups, query_send, 0)
+    query_send(1, 0)
+    lax.fori_loop(1, min(2, chips - 1), ring_next, 0)
+    lax.fori_loop(2, groups, query_send, 0)
     gq_ref[...] = query_part(t)
-    lax.fori_loop(1, chips - 1, ring_next, 0)
+    lax.fori_loop(2, chips - 1, ring_next, 0)
 
     def unnormalized(grad, unit, inverse):
         grad = grad * SCALE
@@ -332,6 +339,23 @@
             if s < chips - 1:
                 ring_copy(s, h).wait_send()
                 rg_copy(s, h).wait_send()
+
+
+PIECES = 4
+
+
+def deliver(loss_in, gq_in, gk_in, loss_out, gq_out, gk_out, sems, loss_sem):
+    part = gq_out.shape[0]
+    start = pl.multiple_of(lax.axis_index("tensor") * part, part)
+    copies = [pltpu.make_async_copy(loss_in.at[:, pl.ds(start, part)], loss_out, loss_sem)]
+    for a, (src, dst) in enumerate(((gq_in, gq_out), (gk_in, gk_out))):
+        for p in range(PIECES):
+            span = pl.ds(p * (part // PIECES), part // PIECES)
+            copies.append(pltpu.make_async_copy(src.at[span], dst.at[span], sems.at[a, p]))
+    for copy in copies:
+        copy.start()
+    for copy in copies:
+        copy.wait()
 
 
 def body(queries, keys, projection, positives):
@@ -388,9 +412,23 @@
             transcendentals=2 * rows * dp * part,
         ),
     )(queries, keys, projection, positives)
-    row_start = lax.axis_index("tensor") * part
-    pair_loss = lax.dynamic_slice_in_dim(loss[0], row_start, part, 0)
-    return (pair_loss, grad_q, grad_k)
+    whole = pl.BlockSpec(memory_space=pl.ANY)
+    pair_loss, grad_q, grad_k = pl.pallas_call(
+        deliver,
+        out_shape=(
+            jax.ShapeDtypeStruct((1, part), f32),
+            jax.ShapeDtypeStruct((part, width), f32),
+            jax.ShapeDtypeStruct((part, width), f32),
+        ),
+        in_specs=[whole] * 3,
+        out_specs=(whole,) * 3,
+        scratch_shapes=[dma((2, PIECES)), dma],
+        compiler_params=pltpu.CompilerParams(vmem_limit_bytes=62 * 1024 * 1024),
+        cost_estimate=pl.CostEstimate(
+            flops=0, bytes_accessed=16 * part * width, transcendentals=0
+        ),
+    )(loss, grad_q, grad_k)
+    return (pair_loss.reshape(part), grad_q, grad_k)
 
 
 def solution(mesh):

time: 64.9 us -> 93.5 us (1.44); the launches traced: 64.6 us -> 92.3 us
  Pallas kernels: 59.1 us -> 91.6 us
  local copies, waits for them, and re-layouts: 4.89 us -> 0 us
    pallas_call x0 -> x1, Pallas kernels: none -> 33 us  [body(): pl.pallas_call(deliver, out_shape=(jax.ShapeDtypeStruct((1, part), f32),...]
    unnamed x2 -> x0, local copies, waits for them, and re-layouts: 3.77 us -> none
    dynamic_slice x1 -> x0, local copies, waits for them, and re-layouts: 1.12 us -> none  [body(): pair_loss = lax.dynamic_slice_in_dim(loss[0], row_start, part, 0)]
where the time goes in v3:
time: 93.5 us; the launch traced here: 92.3 us
  Pallas kernels  91.6 us (98%)
    pallas_call x1, Pallas kernels, body(): pl.pallas_call(functools.partial(kernel, chips, groups), out_shape=(jax.S...  58.7 us
    pallas_call x1, Pallas kernels, body(): pl.pallas_call(deliver, out_shape=(jax.ShapeDtypeStruct((1, part), f32),...  33 us

profile of v3, /device:TPU:0, one launch (start us, length us, event | category | flops | bytes accessed | tf_op | source)
XLA Modules:
  0.0 92.3 jit_solution(6324335065006843939)
XLA Ops:
  0.6 58.7 %shard_map.67 = (f32[1,512]{1,0:T(1,128)}, f32[128,1024]{1,0:T(8,128)}, f32[128,1024]{1,0:T(8,128)}) custom-call(bf16[512,4096]{1,0:T(8,128)(2,1)} %q_hbm.1, bf16[512,4096]{1,0:T(8,128)(2,1)} %k_hbm.1, bf16[4096,256]{1,0:T(8,128)(2,1)} %w_hbm.1, s32[1,512]{1,0:T(1,128)} %pos_ref.1), custom_call_target="tpu_custom_call" | custom-call | flops 6442450944 | bytes 11534336 | tf_op jit(solution)/shard_map/pallas_call | solution.py:373
  59.3 33.0 %shard_map.68 = (f32[1,128]{1,0:T(1,128)}, f32[128,1024]{1,0:T(8,128)}, f32[128,1024]{1,0:T(8,128)}) custom-call(f32[1,512]{1,0:T(1,128)} %get-tuple-element.9.loss_in, f32[128,1024]{1,0:T(8,128)} %get-tuple-element.10.gq_in, f32[128,1024]{1,0:T(8,128)} %get-tuple-element.11.gk_in), custom_call_target="tpu_custom_call" | custom-call | bytes 2097152 | tf_op jit(solution)/shard_map/pallas_call | solution.py:416

commit v4 on v3

--- a/solution.py
+++ b/solution.py
@@ -301,8 +301,8 @@
     query_send(1, 0)
     lax.fori_loop(1, min(2, chips - 1), ring_next, 0)
     lax.fori_loop(2, groups, query_send, 0)
+    lax.fori_loop(2, chips - 1, ring_next, 0)
     gq_ref[...] = query_part(t)
-    lax.fori_loop(2, chips - 1, ring_next, 0)
 
     def unnormalized(grad, unit, inverse):
         grad = grad * SCALE
@@ -344,18 +344,31 @@
 PIECES = 4
 
 
-def deliver(loss_in, gq_in, gk_in, loss_out, gq_out, gk_out, sems, loss_sem):
+def deliver(
+    loss_in, gq_in, gk_in, loss_out, gq_out, gk_out, loss_held, held, in_sems, out_sems, loss_sems
+):
     part = gq_out.shape[0]
     start = pl.multiple_of(lax.axis_index("tensor") * part, part)
-    copies = [pltpu.make_async_copy(loss_in.at[:, pl.ds(start, part)], loss_out, loss_sem)]
+    copies = []
     for a, (src, dst) in enumerate(((gq_in, gq_out), (gk_in, gk_out))):
         for p in range(PIECES):
             span = pl.ds(p * (part // PIECES), part // PIECES)
-            copies.append(pltpu.make_async_copy(src.at[span], dst.at[span], sems.at[a, p]))
-    for copy in copies:
-        copy.start()
-    for copy in copies:
-        copy.wait()
+            slot = held.at[a, span]
+            copies.append((
+                pltpu.make_async_copy(src.at[span], slot, in_sems.at[a, p]),
+                pltpu.make_async_copy(slot, dst.at[span], out_sems.at[a, p]),
+            ))
+    copies.append((
+        pltpu.make_async_copy(loss_in.at[:, pl.ds(start, part)], loss_held, loss_sems.at[0]),
+        pltpu.make_async_copy(loss_held, loss_out, loss_sems.at[1]),
+    ))
+    for arrive, _ in copies:
+        arrive.start()
+    for arrive, leave in copies:
+        arrive.wait()
+        leave.start()
+    for _, leave in copies:
+        leave.wait()
 
 
 def body(queries, keys, projection, positives):
@@ -422,7 +435,10 @@
         ),
         in_specs=[whole] * 3,
         out_specs=(whole,) * 3,
-        scratch_shapes=[dma((2, PIECES)), dma],
+        scratch_shapes=[
+            vmem((1, part), f32), vmem((2, part, width), f32),
+            dma((2, PIECES)), dma((2, PIECES)), dma((2,)),
+        ],
         compiler_params=pltpu.CompilerParams(vmem_limit_bytes=62 * 1024 * 1024),
         cost_estimate=pl.CostEstimate(
             flops=0, bytes_accessed=16 * part * width, transcendentals=0

time: 93.5 us -> 62.6 us (0.67)
  Pallas kernels: 91.6 us -> 60.8 us
    pallas_call x1, Pallas kernels: 33 us -> 2.11 us  [body(): pl.pallas_call(deliver, out_shape=(jax.ShapeDtypeStruct((1, part), f32),...]
where the time goes in v4:
time: 62.6 us; the launch traced here: 61.4 us
  Pallas kernels  60.8 us (97%)
  between operations  0.64 us (1%)
    pallas_call x1, Pallas kernels, body(): pl.pallas_call(functools.partial(kernel, chips, groups), out_shape=(jax.S...  58.7 us
    pallas_call x1, Pallas kernels, body(): pl.pallas_call(deliver, out_shape=(jax.ShapeDtypeStruct((1, part), f32),...  2.11 us

profile of v4, /device:TPU:0, one launch (start us, length us, event | category | flops | bytes accessed | tf_op | source)
XLA Modules:
  0.0 61.4 jit_solution(17544390031084937066)
XLA Ops:
  0.6 58.7 %shard_map.67 = (f32[1,512]{1,0:T(1,128)}, f32[128,1024]{1,0:T(8,128)}, f32[128,1024]{1,0:T(8,128)}) custom-call(bf16[512,4096]{1,0:T(8,128)(2,1)} %q_hbm.1, bf16[512,4096]{1,0:T(8,128)(2,1)} %k_hbm.1, bf16[4096,256]{1,0:T(8,128)(2,1)} %w_hbm.1, s32[1,512]{1,0:T(1,128)} %pos_ref.1), custom_call_target="tpu_custom_call" | custom-call | flops 6442450944 | bytes 11534336 | tf_op jit(solution)/shard_map/pallas_call | solution.py:386
  59.3 2.1 %shard_map.68 = (f32[1,128]{1,0:T(1,128)}, f32[128,1024]{1,0:T(8,128)}, f32[128,1024]{1,0:T(8,128)}) custom-call(f32[1,512]{1,0:T(1,128)} %get-tuple-element.9.loss_in, f32[128,1024]{1,0:T(8,128)} %get-tuple-element.10.gq_in, f32[128,1024]{1,0:T(8,128)} %get-tuple-element.11.gk_in), custom_call_target="tpu_custom_call" | custom-call | bytes 2097152 | tf_op jit(solution)/shard_map/pallas_call | solution.py:429

commit v5 on v4

--- a/solution.py
+++ b/solution.py
@@ -31,8 +31,8 @@
     chip, core = me // 2, me % 2
     other = 1 - core
     sibling = chip * 2 + other
-    right = lax.rem(chip + 1, chips) * 2 + core
-    left = lax.rem(chip + chips - 1, chips) * 2 + core
+    right = lax.rem(chip + chips + 1 - 2 * core, chips) * 2 + core
+    left = lax.rem(chip + chips - 1 + 2 * core, chips) * 2 + core
 
     def peer(i):
         return lax.rem(t + i, groups)
@@ -119,16 +119,16 @@
             jnp.bfloat16
         )
 
-    def source(s):
-        return lax.rem(chip + chips - s, chips) * 2
+    def source(s, c):
+        return lax.rem(chip + chips - s + 2 * s * c, chips) * 2 + c
 
     def ring_copy(s, h):
-        slot = kall.at[source(s) + core, pl.ds(h * half, half)]
-        return remote(slot, slot, ring_send.at[s, h], k_recv.at[source(s) + core, h], (right, t))
+        slot = kall.at[source(s, core), pl.ds(h * half, half)]
+        return remote(slot, slot, ring_send.at[s, h], k_recv.at[source(s, core), h], (right, t))
 
     def fwd_copy(s, h):
-        slot = kall.at[source(s) + core, pl.ds(h * half, half)]
-        return remote(slot, slot, fwd_send.at[s, h], k_recv.at[source(s) + core, h], (sibling, t))
+        slot = kall.at[source(s, core), pl.ds(h * half, half)]
+        return remote(slot, slot, fwd_send.at[s, h], k_recv.at[source(s, core), h], (sibling, t))
 
     def k_from(index, h):
         slot = kall.at[index, pl.ds(h * half, half)]
@@ -137,7 +137,7 @@
     def forward(s):
         for h in range(HALVES):
             if s > 0:
-                k_from(source(s) + core, h).wait_recv()
+                k_from(source(s, core), h).wait_recv()
             if s < chips - 1:
                 ring_copy(s, h).start()
             fwd_copy(s, h).start()
@@ -188,15 +188,15 @@
 
     def from_sibling(s):
         for h in range(HALVES):
-            k_from(source(s) + other, h).wait_recv()
+            k_from(source(s, other), h).wait_recv()
 
     def fold_pair(s, state):
-        state = fold(source(s) + core, state)
+        state = fold(source(s, core), state)
         from_sibling(s)
-        return fold(source(s) + other, state)
+        return fold(source(s, other), state)
 
     from_sibling(0)
-    state = fold(source(0) + other, (row_max, row_sum))
+    state = fold(source(0, other), (row_max, row_sum))
     state = lax.fori_loop(1, chips - 1, fold_pair, state)
     forward(chips - 1)
     row_max, row_sum = fold_pair(chips - 1, state)
@@ -231,8 +231,8 @@
         weights[index] = jnp.exp(scores[index] - log_total).astype(jnp.bfloat16)
         return carried
 
-    def target(i):
-        return lax.rem(chip + 2 * chips - 1 - i, chips) * 2
+    def target(i, c):
+        return lax.rem(chip + 2 * chips - (1 + i) * (1 - 2 * c), chips) * 2 + c
 
     def key_part(index):
         return jnp.dot(weights[index], qhat[...], preferred_element_type=jnp.float32)
@@ -247,12 +247,12 @@
         )
 
     def hand_over(i, carried):
-        sib_out[i] = key_part(target(i) + other).astype(jnp.bfloat16)
+        sib_out[i] = key_part(target(i, other)).astype(jnp.bfloat16)
         sb_copy(i).start()
         return carried
 
     def ring_first():
-        value = key_part(target(0) + core)
+        value = key_part(target(0, core))
         sb_copy(0).wait_recv()
         for h in range(HALVES):
             span = slice(h * half, (h + 1) * half)
@@ -260,7 +260,7 @@
             rg_copy(0, h).start()
 
     def ring_next(i, carried):
-        value = key_part(target(i) + core)
+        value = key_part(target(i, core))
         sb_copy(i).wait_recv()
         for h in range(HALVES):
             span = slice(h * half, (h + 1) * half)
@@ -271,9 +271,9 @@
         return carried
 
     def weigh_pair(i, carried):
-        weigh(target(i) + other, 0)
+        weigh(target(i, other), 0)
         hand_over(i, 0)
-        return weigh(target(i) + core, carried)
+        return weigh(target(i, core), carried)
 
     weigh_pair(0, 0)
     ring_first()

time: 62.6 us -> 64 us (1.022)
  the two profiles are of different devices: /device:TPU:0 before, /device:TPU:3 now
where the time goes in v5:
time: 64 us; the launch traced here: 63.8 us
  Pallas kernels  63.2 us (99%)
  between operations  0.64 us (1%)
    pallas_call x1, Pallas kernels, body(): pl.pallas_call(functools.partial(kernel, chips, groups), out_shape=(jax.S...  61.1 us
    pallas_call x1, Pallas kernels, body(): pl.pallas_call(deliver, out_shape=(jax.ShapeDtypeStruct((1, part), f32),...  2.11 us

profile of v5, /device:TPU:3, one launch (start us, length us, event | category | flops | bytes accessed | tf_op | source)
XLA Modules:
  0.0 63.8 jit_solution(15680733012554243713)
XLA Ops:
  0.6 61.1 %shard_map.67 = (f32[1,512]{1,0:T(1,128)}, f32[128,1024]{1,0:T(8,128)}, f32[128,1024]{1,0:T(8,128)}) custom-call(bf16[512,4096]{1,0:T(8,128)(2,1)} %q_hbm.1, bf16[512,4096]{1,0:T(8,128)(2,1)} %k_hbm.1, bf16[4096,256]{1,0:T(8,128)(2,1)} %w_hbm.1, s32[1,512]{1,0:T(1,128)} %pos_ref.1), custom_call_target="tpu_custom_call" | custom-call | flops 6442450944 | bytes 11534336 | tf_op jit(solution)/shard_map/pallas_call | solution.py:386
  61.7 2.1 %shard_map.68 = (f32[1,128]{1,0:T(1,128)}, f32[128,1024]{1,0:T(8,128)}, f32[128,1024]{1,0:T(8,128)}) custom-call(f32[1,512]{1,0:T(1,128)} %get-tuple-element.9.loss_in, f32[128,1024]{1,0:T(8,128)} %get-tuple-element.10.gq_in, f32[128,1024]{1,0:T(8,128)} %get-tuple-element.11.gk_in), custom_call_target="tpu_custom_call" | custom-call | bytes 2097152 | tf_op jit(solution)/shard_map/pallas_call | solution.py:429

commit v6 on v4

--- a/solution.py
+++ b/solution.py
@@ -10,7 +10,7 @@
 SCALE = 100.0
 EPSILON = 1e-06
 MESH = pl.DeviceIdType.MESH
-HALVES = 2
+SPLITS = 4
 DEPTH = 512
 STAGE_BYTES = 4 * 1024 * 1024
 
@@ -25,7 +25,7 @@
     rows, feats = kfeat.shape
     slots, steps = stage.shape[0], w_in.shape[0] // DEPTH
     part = rows // groups
-    half = part // HALVES
+    piece = part // SPLITS
     me = lax.axis_index("dp")
     t = lax.axis_index("tensor")
     chip, core = me // 2, me % 2
@@ -123,19 +123,19 @@
         return lax.rem(chip + chips - s, chips) * 2
 
     def ring_copy(s, h):
-        slot = kall.at[source(s) + core, pl.ds(h * half, half)]
+        slot = kall.at[source(s) + core, pl.ds(h * piece, piece)]
         return remote(slot, slot, ring_send.at[s, h], k_recv.at[source(s) + core, h], (right, t))
 
     def fwd_copy(s, h):
-        slot = kall.at[source(s) + core, pl.ds(h * half, half)]
+        slot = kall.at[source(s) + core, pl.ds(h * piece, piece)]
         return remote(slot, slot, fwd_send.at[s, h], k_recv.at[source(s) + core, h], (sibling, t))
 
     def k_from(index, h):
-        slot = kall.at[index, pl.ds(h * half, half)]
+        slot = kall.at[index, pl.ds(h * piece, piece)]
         return remote(slot, slot, ring_send.at[0, h], k_recv.at[index, h], (right, t))
 
     def forward(s):
-        for h in range(HALVES):
+        for h in range(SPLITS):
             if s > 0:
                 k_from(source(s) + core, h).wait_recv()
             if s < chips - 1:
@@ -187,7 +187,7 @@
     matched = jnp.sum(own * positive_mask(), axis=0, keepdims=True)
 
     def from_sibling(s):
-        for h in range(HALVES):
+        for h in range(SPLITS):
             k_from(source(s) + other, h).wait_recv()
 
     def fold_pair(s, state):
@@ -241,7 +241,7 @@
         return remote(sib_out.at[i], sib_in.at[i], sb_send.at[i], sb_recv.at[i], (sibling, t))
 
     def rg_copy(i, h):
-        span = pl.ds(h * half, half)
+        span = pl.ds(h * piece, piece)
         return remote(
             sib_in.at[i, span], ring_in.at[i, span], rg_send.at[i, h], rg_recv.at[i, h], (right, t)
         )
@@ -254,16 +254,16 @@
     def ring_first():
         value = key_part(target(0) + core)
         sb_copy(0).wait_recv()
-        for h in range(HALVES):
-            span = slice(h * half, (h + 1) * half)
+        for h in range(SPLITS):
+            span = slice(h * piece, (h + 1) * piece)
             sib_in[0, span] = (value[span] + sib_in[0, span].astype(jnp.float32)).astype(jnp.bfloat16)
             rg_copy(0, h).start()
 
     def ring_next(i, carried):
         value = key_part(target(i) + core)
         sb_copy(i).wait_recv()
-        for h in range(HALVES):
-            span = slice(h * half, (h + 1) * half)
+        for h in range(SPLITS):
+            span = slice(h * piece, (h + 1) * piece)
             both = value[span] + sib_in[i, span].astype(jnp.float32)
             rg_copy(i - 1, h).wait_recv()
             sib_in[i, span] = (both + ring_in[i - 1, span].astype(jnp.float32)).astype(jnp.bfloat16)
@@ -320,7 +320,7 @@
     value = key_part(me)
     sb_copy(chips - 1).wait_recv()
     value = value + sib_in[chips - 1].astype(jnp.float32)
-    for h in range(HALVES):
+    for h in range(SPLITS):
         rg_copy(chips - 2, h).wait_recv()
     value = value + ring_in[chips - 2].astype(jnp.float32)
     blocks = [kraw[s].astype(jnp.float32) for s in range(groups)]
@@ -334,7 +334,7 @@
         gq_copy(i).wait_send()
     for s in range(chips):
         sb_copy(s).wait_send()
-        for h in range(HALVES):
+        for h in range(SPLITS):
             fwd_copy(s, h).wait_send()
             if s < chips - 1:
                 ring_copy(s, h).wait_send()
@@ -410,10 +410,10 @@
             vmem((groups - 1, part, width), bf16),
             dma((slots,)), dma((embed // DEPTH,)),
             dma((groups,)), dma((groups,)), dma((groups,)), dma((groups,)),
-            dma((chips, HALVES)), dma((chips, HALVES)), dma((dp, HALVES)),
+            dma((chips, SPLITS)), dma((chips, SPLITS)), dma((dp, SPLITS)),
             dma((groups,)), dma((groups,)),
             dma((chips,)), dma((chips,)),
-            dma((chips, HALVES)), dma((chips, HALVES)),
+            dma((chips, SPLITS)), dma((chips, SPLITS)),
             dma((groups,)), dma((groups,)),
         ],
         compiler_params=pltpu.CompilerParams(

time: 62.6 us -> 63.1 us (level)
  no operation moved by 1% of the time
where the time goes in v6:
time: 63.1 us; the launch traced here: 61.9 us
  Pallas kernels  61.2 us (97%)
  between operations  0.64 us (1%)
    pallas_call x1, Pallas kernels, body(): pl.pallas_call(functools.partial(kernel, chips, groups), out_shape=(jax.S...  59.1 us
    pallas_call x1, Pallas kernels, body(): pl.pallas_call(deliver, out_shape=(jax.ShapeDtypeStruct((1, part), f32),...  2.11 us

profile of v6, /device:TPU:0, one launch (start us, length us, event | category | flops | bytes accessed | tf_op | source)
XLA Modules:
  0.0 61.9 jit_solution(16221746961041216194)
XLA Ops:
  0.6 59.1 %shard_map.67 = (f32[1,512]{1,0:T(1,128)}, f32[128,1024]{1,0:T(8,128)}, f32[128,1024]{1,0:T(8,128)}) custom-call(bf16[512,4096]{1,0:T(8,128)(2,1)} %q_hbm.1, bf16[512,4096]{1,0:T(8,128)(2,1)} %k_hbm.1, bf16[4096,256]{1,0:T(8,128)(2,1)} %w_hbm.1, s32[1,512]{1,0:T(1,128)} %pos_ref.1), custom_call_target="tpu_custom_call" | custom-call | flops 6442450944 | bytes 11534336 | tf_op jit(solution)/shard_map/pallas_call | solution.py:386
  59.8 2.1 %shard_map.68 = (f32[1,128]{1,0:T(1,128)}, f32[128,1024]{1,0:T(8,128)}, f32[128,1024]{1,0:T(8,128)}) custom-call(f32[1,512]{1,0:T(1,128)} %get-tuple-element.9.loss_in, f32[128,1024]{1,0:T(8,128)} %get-tuple-element.10.gq_in, f32[128,1024]{1,0:T(8,128)} %get-tuple-element.11.gk_in), custom_call_target="tpu_custom_call" | custom-call | bytes 2097152 | tf_op jit(solution)/shard_map/pallas_call | solution.py:429

commit v7 on v4

--- a/solution.py
+++ b/solution.py
@@ -298,9 +298,8 @@
         gq_copy(i).start()
         return carried
 
-    query_send(1, 0)
     lax.fori_loop(1, min(2, chips - 1), ring_next, 0)
-    lax.fori_loop(2, groups, query_send, 0)
+    lax.fori_loop(1, groups, query_send, 0)
     lax.fori_loop(2, chips - 1, ring_next, 0)
     gq_ref[...] = query_part(t)
 

time: 62.6 us -> 65 us (1.038); the launches traced: 61.4 us -> 64.9 us
  Pallas kernels: 60.8 us -> 64.2 us
    pallas_call x1, Pallas kernels: 58.7 us -> 62.1 us  [body(): pl.pallas_call(functools.partial(kernel, chips, groups), out_shape=(jax.S...]
where the time goes in v7:
time: 65 us; the launch traced here: 64.9 us
  Pallas kernels  64.2 us (99%)
    pallas_call x1, Pallas kernels, body(): pl.pallas_call(functools.partial(kernel, chips, groups), out_shape=(jax.S...  62.1 us
    pallas_call x1, Pallas kernels, body(): pl.pallas_call(deliver, out_shape=(jax.ShapeDtypeStruct((1, part), f32),...  2.11 us

profile of v7, /device:TPU:0, one launch (start us, length us, event | category | flops | bytes accessed | tf_op | source)
XLA Modules:
  0.0 64.9 jit_solution(16392907704819616806)
XLA Ops:
  0.6 62.1 %shard_map.67 = (f32[1,512]{1,0:T(1,128)}, f32[128,1024]{1,0:T(8,128)}, f32[128,1024]{1,0:T(8,128)}) custom-call(bf16[512,4096]{1,0:T(8,128)(2,1)} %q_hbm.1, bf16[512,4096]{1,0:T(8,128)(2,1)} %k_hbm.1, bf16[4096,256]{1,0:T(8,128)(2,1)} %w_hbm.1, s32[1,512]{1,0:T(1,128)} %pos_ref.1), custom_call_target="tpu_custom_call" | custom-call | flops 6442450944 | bytes 11534336 | tf_op jit(solution)/shard_map/pallas_call | solution.py:385
  62.8 2.1 %shard_map.68 = (f32[1,128]{1,0:T(1,128)}, f32[128,1024]{1,0:T(8,128)}, f32[128,1024]{1,0:T(8,128)}) custom-call(f32[1,512]{1,0:T(1,128)} %get-tuple-element.9.loss_in, f32[128,1024]{1,0:T(8,128)} %get-tuple-element.10.gq_in, f32[128,1024]{1,0:T(8,128)} %get-tuple-element.11.gk_in), custom_call_target="tpu_custom_call" | custom-call | bytes 2097152 | tf_op jit(solution)/shard_map/pallas_call | solution.py:428
